TPU v7x, 512 devices: a whole 4x4x16 slice. The times are simulated.
512 devices in a mesh: fsdp: 128 (over y, z, core), rep: 4 (over x).
Axes of the slice: x: 4, y: 4, z: 16, core: 2. Of those that a mesh axis runs over, the one named last changes fastest.
Arguments:
- partials: bfloat16 [4, 8192, 8192], P('rep', 'fsdp'), may hold values from -20 to 20
- factor_stats: float32 [128, 4, 512, 512], P('fsdp', 'rep'), may hold values from -64 to 34816, as said below
- owner_slots: int32 [256], replicated, may hold values from 0 to 255, each once
Outputs:
- update: bfloat16 [8192, 8192], P(('fsdp', 'rep'))
Inputs may be any that keep to these rules, and one draw needn't show every extreme that they name: `owner_slots`: every pair slot owns exactly one block. Each matrix factor_stats[o, r] is symmetric with a positive diagonal that exceeds the sum of the magnitudes of the other entries of its row.
All inputs are finite; a program needn't handle non-finite values.
Results may differ from a plain program's by a relative error of at most 0.015.
Values may be sent and summed in bfloat16 or wider, within the bound.
No kernel may reach another device: no remote copies, remote signals or barrier semaphores. Data moves between devices by JAX's collectives and lax.ppermute only.
A program may use at most 64 MiB of HBM per device.

v0:
```python
import jax
import jax.numpy as jnp
from jax import lax
from jax.sharding import PartitionSpec as P

ITERS = 2
POWER_STEPS = 6


HIGHEST = lax.Precision.HIGHEST
EPSILON = 1e-06


def from_partner(block, axis, stride):
    count = lax.axis_size(axis)
    route = []
    for low in range(count):
        high = low | 1 << stride
        if high != low and high < count:
            route += [(low, high), (high, low)]
    return lax.ppermute(block, axis, route)


def inverse_fourth_root(statistic):
    order_size = statistic.shape[0]
    identity = jnp.eye(order_size, dtype=jnp.float32)
    vector = jnp.ones((order_size,), jnp.float32)
    for power_step in range(POWER_STEPS):
        image = jnp.dot(statistic, vector, precision=HIGHEST)
        vector = image * lax.rsqrt(jnp.sum(image * image) + EPSILON)
    largest = jnp.sum(vector * jnp.dot(statistic, vector, precision=HIGHEST))
    matrix = statistic / largest
    inverse_root = identity
    for newton_step in range(ITERS):
        factor = (5.0 * identity - matrix) * 0.25
        inverse_root = jnp.dot(inverse_root, factor, precision=HIGHEST)
        if newton_step + 1 < ITERS:
            square = jnp.dot(factor, factor, precision=HIGHEST)
            fourth = jnp.dot(square, square, precision=HIGHEST)
            matrix = jnp.dot(fourth, matrix, precision=HIGHEST)
    return inverse_root


def on_device(partials, factor_stats, owner_slots):
    rep_count = lax.axis_size("rep")
    fsdp_count = lax.axis_size("fsdp")
    rep_index = lax.axis_index("rep")
    fsdp_index = lax.axis_index("fsdp")
    pair_count = rep_count // 2
    rows_dev = partials.shape[1]
    model_width = partials.shape[2]
    block_order = factor_stats.shape[-1]
    column_count = model_width // block_order
    band_span = block_order // rows_dev
    band_total = fsdp_count // band_span
    quarter = rows_dev // rep_count
    half_order = block_order // 2
    block_count = owner_slots.shape[0]
    factor_side = rep_index % 2
    pair_index = rep_index // 2
    positions = jnp.arange(block_count, dtype=jnp.int32)
    first_rows = []
    for member in range(pair_count):
        slot_index = fsdp_index * pair_count + member
        block_index = jnp.sum(jnp.where(owner_slots == slot_index, positions, 0))
        first_rows.append(block_index // column_count * band_span)
    partial_value = partials[0].astype(jnp.float32)
    summed = lax.psum(partial_value.astype(jnp.bfloat16), "rep")
    piece_width = rows_dev * block_order // fsdp_count
    layout = summed.reshape(rows_dev, column_count, block_order).transpose(1, 0, 2)
    layout = layout.reshape(column_count, fsdp_count, piece_width).transpose(1, 0, 2)
    spread = lax.all_to_all(layout, "fsdp", split_axis=0, concat_axis=0, tiled=True)
    by_block = spread.reshape(band_total, band_span, column_count, piece_width).transpose(
        0, 2, 1, 3
    )
    by_block = by_block.reshape(block_count, band_span * piece_width)
    wanted = jnp.arange(fsdp_count, dtype=jnp.int32) * pair_count + pair_index
    dest_select = (owner_slots[None, :] == wanted[:, None]).astype(jnp.bfloat16)
    outgoing = jnp.dot(dest_select, by_block, preferred_element_type=jnp.float32).astype(
        jnp.bfloat16
    )
    received = lax.all_to_all(outgoing, "fsdp", split_axis=0, concat_axis=0, tiled=True)
    gradient = (
        received.reshape(fsdp_count, band_span, piece_width)
        .transpose(1, 0, 2)
        .reshape(block_order, block_order)
    )
    gradient_wide = gradient.astype(jnp.float32)
    own_stat = factor_stats[0, 0]
    partner_stat = from_partner(own_stat.astype(jnp.bfloat16), "rep", 0).astype(own_stat.dtype)
    left_old = jnp.where(factor_side == 0, own_stat, partner_stat)
    right_old = jnp.where(factor_side == 0, partner_stat, own_stat)
    left_root = inverse_fourth_root(
        left_old + jnp.dot(gradient, gradient.T, preferred_element_type=jnp.float32)
    )
    right_root = inverse_fourth_root(
        right_old + jnp.dot(gradient.T, gradient, preferred_element_type=jnp.float32)
    )
    product = jnp.dot(
        jnp.dot(left_root, gradient_wide, precision=HIGHEST), right_root, precision=HIGHEST
    )
    total_squares = jnp.sum(product * product)
    rows_part = lax.dynamic_slice_in_dim(product, factor_side * half_order, half_order, 0)
    graft_scale = jnp.sqrt(jnp.sum(gradient_wide * gradient_wide) + EPSILON) * lax.rsqrt(
        total_squares + EPSILON
    )
    update_rows = (rows_part * graft_scale).astype(jnp.bfloat16)
    arranged = update_rows.reshape(band_span // 2, rep_count, quarter, block_order).transpose(
        1, 0, 2, 3
    )
    regrouped = lax.all_to_all(arranged, "rep", split_axis=0, concat_axis=0, tiled=True)
    regrouped = regrouped.reshape(pair_count, band_span, quarter, block_order)
    piece_back = quarter * block_order // fsdp_count
    sending = regrouped.reshape(pair_count, band_span, fsdp_count, piece_back).transpose(2, 0, 1, 3)
    gathered_back = lax.all_to_all(sending, "fsdp", split_axis=0, concat_axis=0, tiled=True)
    by_slot = gathered_back.reshape(block_count, band_span * piece_back)
    slot_select = (owner_slots[:, None] == positions[None, :]).astype(jnp.bfloat16)
    by_block_back = jnp.dot(slot_select, by_slot, preferred_element_type=jnp.float32).astype(
        jnp.bfloat16
    )
    toward = by_block_back.reshape(band_total, column_count, band_span, piece_back).transpose(
        0, 2, 1, 3
    )
    toward = toward.reshape(fsdp_count, column_count * piece_back)
    arrived = lax.all_to_all(toward, "fsdp", split_axis=0, concat_axis=0, tiled=True)
    arrived = arrived.reshape(fsdp_count, column_count, piece_back).transpose(1, 0, 2)
    mixed = arrived.reshape(column_count, quarter, block_order).transpose(1, 0, 2)
    return mixed.reshape(quarter, model_width)


def solution(mesh):
    return jax.shard_map(
        on_device,
        mesh=mesh,
        in_specs=(P("rep", "fsdp", None), P("fsdp", "rep", None, None), P()),
        out_specs=P(("fsdp", "rep"), None),
        check_vma=False,
    )
```

profile of v0, /device:TPU:1, one launch (start us, length us, event | category | flops | bytes accessed | tf_op | source)
XLA Modules:
  0.0 349.4 jit_solution(12381382955079542169)
XLA Ops:
  6.5 1.6 copy.47
  10.0 65.3 %all-reduce.2.cloned.1.call-done = bf16[128,16,256]{2,0,1:T(8,128)(2,1)} async-done(((bf16[128,16,256]{2,0,1:T(8,128)(2,1)}), bf16[128,16,256]{2,0,1:T(8,128)(2,1)}) %all-reduce.2.cloned.1.call-update) | async-done | bytes 1048592 | tf_op jit(solution)/shard_map/psum | solution.py:68
  75.2 2.8 copy.34
  78.1 18.0 %all-to-all-start = ((bf16[128,16,256]{2,1,0:T(8,128)(2,1)}), bf16[128,16,256]{2,1,0:T(8,128)(2,1)S(1)}, u32[]{:S(2)}, u32[]{:S(2)}) async-start(bf16[128,16,256]{2,1,0:T(8,128)(2,1)} %copy.34), calls=%async_computation | async-start | bytes 2097152 | tf_op jit(solution)/shard_map/all_to_all | solution.py:72
  96.1 54.3 %all-to-all-done = bf16[128,16,256]{2,1,0:T(8,128)(2,1)S(1)} async-done(((bf16[128,16,256]{2,1,0:T(8,128)(2,1)}), bf16[128,16,256]{2,1,0:T(8,128)(2,1)S(1)}, u32[]{:S(2)}, u32[]{:S(2)}) %all-to-all-start) | async-done | bytes 1048608 | tf_op jit(solution)/shard_map/all_to_all | solution.py:72
  154.9 8.5 %all-to-all-start.1 = ((bf16[128,2,1024]{2,1,0:T(2,128)(2,1)}), bf16[128,2,1024]{2,1,0:T(2,128)(2,1)S(1)}, u32[]{:S(2)}, u32[]{:S(2)}) async-start(bf16[128,2,1024]{2,1,0:T(2,128)(2,1)} %reshape.92), calls=%async_computation.1 | async-start | bytes 1048576 | tf_op jit(solution)/shard_map/all_to_all | solution.py:82
  163.5 2.3 collective-permute-start
  165.8 30.8 %all-to-all-done.1 = bf16[128,2,1024]{2,1,0:T(2,128)(2,1)S(1)} async-done(((bf16[128,2,1024]{2,1,0:T(2,128)(2,1)}), bf16[128,2,1024]{2,1,0:T(2,128)(2,1)S(1)}, u32[]{:S(2)}, u32[]{:S(2)}) %all-to-all-start.1) | async-done | bytes 524320 | tf_op jit(solution)/shard_map/all_to_all | solution.py:82
  197.0 1.4 copy.37
  217.6 3.6 %fusion.12 = f32[512,512]{1,0:T(8,128)} fusion(f32[512,512]{1,0:T(8,128)S(1)} %get-tuple-element.6, f32[]{:T(128)} %multiply_reduce_fusion.9), kind=kOutput, calls=%fused_computation.23 | convolution fusion | flops 1611923456 | bytes 2097156 | tf_op jit(solution)/shard_map/dot_general | solution.py:38
  221.2 2.8 fusion.8
  239.6 3.7 %fusion.9 = f32[512,512]{1,0:T(8,128)} fusion(f32[512,512]{1,0:T(8,128)S(1)} %get-tuple-element.5, f32[]{:T(128)} %multiply_reduce_fusion.2), kind=kOutput, calls=%fused_computation.22 | convolution fusion | flops 1611923456 | bytes 2097156 | tf_op jit(solution)/shard_map/dot_general | solution.py:38
  243.2 2.9 fusion.7
  246.8 3.5 %fusion.56 = f32[512,512]{1,0:T(8,128)S(1)} fusion(f32[512,512]{1,0:T(8,128)} %fusion.12), kind=kOutput, calls=%fused_computation.98 | convolution fusion | flops 1610612736 | bytes 2097152 | tf_op jit(solution)/shard_map/dot_general | solution.py:39
  250.3 2.6 fusion.1
  252.9 1.8 fusion.57
  255.9 2.1 fusion.65
  258.0 2.6 fusion.2
  260.7 1.8 fusion.66
  262.5 2.7 multiply_reduce_fusion
  266.0 8.9 %all_to_all.34 = bf16[4,4,16,512]{3,2,1,0:T(8,128)(2,1)S(1)} all-to-all(bf16[4,4,16,512]{3,2,1,0:T(8,128)(2,1)S(1)} %bitcast.127), channel_id=1, replica_groups=mesh['fsdp'=128,'rep'=4] {'rep'}, dimensions={0} | all-to-all | bytes 524288 | tf_op jit(solution)/shard_map/all_to_all | solution.py:111
  275.8 30.9 %all_to_all.35 = bf16[128,2,512]{2,1,0:T(2,128)(2,1)S(1)} all-to-all(bf16[128,2,512]{2,1,0:T(2,128)(2,1)S(1)} %reshape.94), channel_id=1, replica_groups=mesh['fsdp'=128,'rep'=4] {'fsdp'}, dimensions={0} | all-to-all | bytes 524288 | tf_op jit(solution)/shard_map/all_to_all | solution.py:115
  308.4 2.2 reduce.2
  310.8 29.5 %all_to_all.36 = bf16[128,2,512]{2,1,0:T(2,128)(2,1)S(1)} all-to-all(bf16[128,2,512]{2,1,0:T(2,128)(2,1)S(1)} %reshape.96), channel_id=1, replica_groups=mesh['fsdp'=128,'rep'=4] {'fsdp'}, dimensions={0} | all-to-all | bytes 524288 | tf_op jit(solution)/shard_map/all_to_all | solution.py:125
  (89 shorter events, 39.0 us)
Async XLA Ops:
  6.5 68.7 %all-reduce.2.cloned.1.call-start = ((), (), s32[]{:S(2)}) async-start(), calls=%async_computation.5 | async-start | bytes 2097152 | tf_op jit(solution)/shard_map/psum | solution.py:68
  78.1 72.4 %all-to-all-start = ((bf16[128,16,256]{2,1,0:T(8,128)(2,1)}), bf16[128,16,256]{2,1,0:T(8,128)(2,1)S(1)}, u32[]{:S(2)}, u32[]{:S(2)}) async-start(bf16[128,16,256]{2,1,0:T(8,128)(2,1)} %copy.34), calls=%async_computation | async-start | bytes 2097152 | tf_op jit(solution)/shard_map/all_to_all | solution.py:72
  151.2 0.7 copy-start.5
  153.7 9.7 %copy-start.1 = (f32[1,1,512,512]{3,2,1,0:T(8,128)S(1)}, f32[1,1,512,512]{3,2,1,0:T(8,128)}, u32[]{:S(2)}) copy-start(f32[1,1,512,512]{3,2,1,0:T(8,128)} %param.4) | copy-start | bytes 3145732
  154.9 41.7 %all-to-all-start.1 = ((bf16[128,2,1024]{2,1,0:T(2,128)(2,1)}), bf16[128,2,1024]{2,1,0:T(2,128)(2,1)S(1)}, u32[]{:S(2)}, u32[]{:S(2)}) async-start(bf16[128,2,1024]{2,1,0:T(2,128)(2,1)} %reshape.92), calls=%async_computation.1 | async-start | bytes 1048576 | tf_op jit(solution)/shard_map/all_to_all | solution.py:82
  163.5 36.7 %collective-permute-start = (bf16[512,512]{1,0:T(8,128)(2,1)S(1)}, bf16[512,512]{1,0:T(8,128)(2,1)S(1)}, u32[]{:S(2)}, u32[]{:S(2)}) collective-permute-start(bf16[512,512]{1,0:T(8,128)(2,1)S(1)} %bitcast_convert_fusion), channel_id=1, source_target_pairs={{0,1},{1,0},{2,3},{3,2},{4,5},{5,4},{6,7},{7,6},{8,9},{9,8},{10,11... | collective-permute-start | bytes 1572872 | tf_op jit(solution)/shard_map/ppermute | solution.py:21
  199.7 1.2 copy-start.2
  250.3 2.6 copy-start.3
  254.7 1.2 copy-start
  258.0 2.7 copy-start.4
Sparse Core Ops, SparseCore 0:
  10.1 65.1 all-reduce.1
where the time goes:
time: 356 us; the launch traced here: 349 us
  waiting for transfers between devices  150 us (42%)
  blocking collectives  69.3 us (19%)
  matrix products  46.5 us (13%)
  starting transfers between devices  28.8 us (8%)
  between operations  23.9 us (7%)
  local copies, waits for them, and re-layouts  17 us (5%)
  other arithmetic  13.5 us (4%)
    psum x1, waiting for transfers between devices, on_device(): summed = lax.psum(partial_value.astype(jnp.bfloat16), 'rep')  65.3 us
    all_to_all x1, waiting for transfers between devices, on_device(): lax.all_to_all(layout, 'fsdp', split_axis=0, concat_axis=0, tiled=True)  54.3 us
    all_to_all x1, blocking collectives, on_device(): lax.all_to_all(sending, 'fsdp', split_axis=0, concat_axis=0, tiled=True)  30.9 us
    all_to_all x1, waiting for transfers between devices, on_device(): lax.all_to_all(outgoing, 'fsdp', split_axis=0, concat_axis=0, tiled=True)  30.8 us
    all_to_all x1, blocking collectives, on_device(): lax.all_to_all(toward, 'fsdp', split_axis=0, concat_axis=0, tiled=True)  29.5 us
    all_to_all x1, starting transfers between devices, on_device(): lax.all_to_all(layout, 'fsdp', split_axis=0, concat_axis=0, tiled=True)  18 us
    dot_general x12, matrix products, inverse_fourth_root(): image = jnp.dot(statistic, vector, precision=HIGHEST)  12 us
    dot_general x4, matrix products, inverse_fourth_root(): inverse_root = jnp.dot(inverse_root, factor, precision=HIGHEST)  9.35 us
  transfers between devices with their start and end apart: 4, of which 3 were waited for; matrix products, arithmetic and copies ran while one was open for 1% of the time, Pallas kernels for 0%

commit v1 on v0

v1 whole, which is shorter than its diff:
```python
import jax
import jax.numpy as jnp
from jax import lax
from jax.experimental import pallas as pl
from jax.experimental.pallas import tpu as pltpu
from jax.sharding import Mesh
from jax.sharding import PartitionSpec as P

POWER_STEPS = 6
EPSILON = 1e-06

PLANE = ("y", "zq", "zl", "core")
EVERYONE = PLANE + ("rep",)

BF16 = jnp.bfloat16
F32 = jnp.float32


def matmul(a, b, contract=((1,), (0,))):
    return lax.dot_general(a, b, (contract, ((), ())), preferred_element_type=F32)


def grid_of(shape):
    return (
        lax.broadcasted_iota(jnp.int32, shape, 0),
        lax.broadcasted_iota(jnp.int32, shape, 1),
    )


def pack_statistic(stat):
    half = stat.shape[0] // 2
    first, cross, last = stat[:half, :half], stat[:half, half:], stat[half:, half:]
    row, col = grid_of((half, half))
    folded = jnp.where(row <= col, first, last)
    diagonal = jnp.sum(jnp.where(row == col, last, 0.0), axis=0)
    packed = jnp.concatenate([folded, cross], axis=1).astype(BF16)
    return packed, diagonal.astype(BF16)


def select_kernel(source_ref, table_ref, out_ref):
    count = out_ref.shape[0]

    def body(index, carry):
        out_ref[index] = table_ref[source_ref[index]]
        return carry

    lax.fori_loop(0, count, body, 0, unroll=16)


def select_rows(source, table):
    return pl.pallas_call(
        select_kernel,
        out_shape=jax.ShapeDtypeStruct(table.shape, table.dtype),
        in_specs=[
            pl.BlockSpec(memory_space=pltpu.SMEM),
            pl.BlockSpec(memory_space=pltpu.VMEM),
        ],
        out_specs=pl.BlockSpec(memory_space=pltpu.VMEM),
        name="select_rows",
    )(source, table)


def unfold(packed_ref, diagonal, stat_ref):
    half = packed_ref.shape[0]
    folded = packed_ref[:, :half].astype(F32)
    cross = packed_ref[:, half:].astype(F32)
    row, col = grid_of((half, half))
    turned = folded.T
    stat_ref[:half, :half] += jnp.where(row <= col, folded, turned)
    lower = jnp.where(row > col, folded, turned)
    stat_ref[half:, half:] += jnp.where(row == col, diagonal, lower)
    stat_ref[:half, half:] += cross
    stat_ref[half:, :half] += cross.T


def main_kernel(
    place_ref, packed_ref, diagonals_ref, pieces_ref, out_ref, grad_ref, left_ref, right_ref
):
    core, zl = place_ref[0], place_ref[1]
    cores, steps, rows, size = pieces_ref.shape
    for step in range(steps):
        origin = lax.rem(zl - step + steps, steps)
        for member in range(cores):
            first = pl.multiple_of((origin * cores + member) * rows, rows)
            grad_ref[pl.ds(first, rows), :] = pieces_ref[member, step]
    gradient = grad_ref[...]
    left_ref[...] = matmul(gradient, gradient, ((1,), (1,)))
    right_ref[...] = matmul(gradient.T, gradient)
    unfold(packed_ref.at[0], diagonals_ref[0:1, :].astype(F32), left_ref)
    unfold(packed_ref.at[1], diagonals_ref[1:2, :].astype(F32), right_ref)
    roots = []
    row, col = grid_of((size, size))
    identity = jnp.where(row == col, 1.0, 0.0)
    images = [jnp.sum(ref[...], axis=0, keepdims=True) for ref in (left_ref, right_ref)]
    for power_step in range(POWER_STEPS):
        vectors = [image * lax.rsqrt(jnp.sum(image * image) + EPSILON) for image in images]
        axis = 1 - power_step % 2
        images = [
            jnp.sum(ref[...] * vector, axis=axis, keepdims=True)
            for ref, vector in zip((left_ref, right_ref), vectors)
        ]
    for ref, vector, image in zip((left_ref, right_ref), vectors, images):
        turned = jnp.sum(identity * vector, axis=0, keepdims=True)
        largest = jnp.sum(turned * image)
        scaled = ref[...] * (1.0 / largest)
        narrow = scaled.astype(BF16)
        second = matmul(narrow, narrow)
        square = (25.0 / 16.0) * identity - (10.0 / 16.0) * scaled + (1.0 / 16.0) * second
        times = (1.25 * scaled - 0.25 * second).astype(BF16)
        narrow = square.astype(BF16)
        fourth = matmul(narrow, narrow).astype(BF16)
        last = matmul(fourth, times)
        roots.append((25.0 / 16.0) * identity - (5.0 / 16.0) * scaled - 0.25 * last)
    left, right = roots
    half_way = matmul(left.astype(BF16), gradient)
    raw = matmul(half_way.astype(BF16), right.astype(BF16))
    wide = gradient.astype(F32)
    scale = jnp.sqrt(jnp.sum(wide * wide) + EPSILON) * lax.rsqrt(
        jnp.sum(raw * raw) + EPSILON
    )
    left_ref[...] = raw * scale
    for origin in range(steps):
        first = pl.multiple_of(origin * cores * rows + core * rows, rows)
        out_ref[origin] = left_ref[pl.ds(first, rows), :].astype(BF16)


def precondition(place, packed, diagonals, pieces):
    size = pieces.shape[-1]
    vmem = pl.BlockSpec(memory_space=pltpu.VMEM)
    return pl.pallas_call(
        main_kernel,
        out_shape=jax.ShapeDtypeStruct(pieces.shape[1:], BF16),
        in_specs=[pl.BlockSpec(memory_space=pltpu.SMEM), vmem, vmem, vmem],
        out_specs=vmem,
        scratch_shapes=[
            pltpu.VMEM((size, size), BF16),
            pltpu.VMEM((size, size), F32),
            pltpu.VMEM((size, size), F32),
        ],
        compiler_params=pltpu.CompilerParams(vmem_limit_bytes=40 * 2**20),
        name="precondition",
    )(place, packed, diagonals, pieces)


def on_device(partials, factor_stats, owner_slots):
    rows, width = partials.shape[1:]
    size = factor_stats.shape[-1]
    reps, zls, cores = (lax.axis_size(name) for name in ("rep", "zl", "core"))
    everyone = lax.axis_size(EVERYONE)
    me = lax.axis_index(EVERYONE)
    core, zl, rep = (lax.axis_index(name) for name in ("core", "zl", "rep"))

    source = 2 * owner_slots.reshape(-1, 1, reps) + jnp.arange(2, dtype=jnp.int32)[None, :, None]
    source = source.reshape(everyone)

    parts = partials[0].reshape(rows, zls, reps, size).transpose(2, 1, 0, 3)
    summed = lax.psum_scatter(parts, "rep", scatter_dimension=0, tiled=False)

    packed, diagonal = pack_statistic(factor_stats[0, 0])
    both = source.reshape(-1, 2, reps)
    both = jnp.broadcast_to(both.transpose(0, 2, 1)[:, None], (both.shape[0], cores, reps, 2))
    mine = both.reshape(everyone, 2) == me
    diagonals = lax.psum_scatter(
        jnp.where(mine[:, :, None], diagonal, jnp.zeros((), BF16)),
        EVERYONE,
        scatter_dimension=0,
        tiled=False,
    )
    tiles = packed.reshape(size // 16, 4, 2, size // 128, 128).transpose(0, 3, 1, 2, 4)
    spread = lax.all_to_all(
        tiles.reshape(everyone, 2, 128), EVERYONE, split_axis=0, concat_axis=0, tiled=True
    )
    outgoing = select_rows(source, spread)
    delivered = lax.all_to_all(outgoing, EVERYONE, split_axis=0, concat_axis=0, tiled=True)
    delivered = delivered.reshape(size // 16, size // 128, 4, 2, 128).transpose(0, 2, 3, 1, 4)
    delivered = delivered.reshape(size // 2, size)

    pieces = [lax.dynamic_index_in_dim(summed, zl, 0, keepdims=False)]
    for step in range(1, zls):
        piece = lax.dynamic_index_in_dim(summed, (zl + step) % zls, 0, keepdims=False)
        route = [(index, (index + step) % zls) for index in range(zls)]
        pieces.append(lax.ppermute(piece, "zl", route))
    pieces = lax.all_gather(jnp.stack(pieces), "core")
    delivered = lax.all_gather(delivered, "core")

    place = jnp.stack([core, zl]).astype(jnp.int32)
    update = precondition(place, delivered, diagonals, pieces)

    update = update.reshape(zls * reps, rows // reps, size)
    arrived = lax.all_to_all(update, ("zl", "rep"), split_axis=0, concat_axis=0, tiled=True)
    return arrived.transpose(1, 0, 2).reshape(rows // reps, width)


def solution(mesh):
    fsdp, reps = mesh.devices.shape
    fine = Mesh(mesh.devices.reshape(4, 4, fsdp // 32, 2, reps), EVERYONE)
    return jax.shard_map(
        on_device,
        mesh=fine,
        in_specs=(P("rep", PLANE, None), P(PLANE, "rep", None, None), P()),
        out_specs=P(EVERYONE, None),
        check_vma=False,
    )
```

time: 356 us -> 532 us (1.49); the launches traced: 349 us -> 532 us
  waiting for transfers between devices: 150 us -> 429 us
  matrix products: 46.5 us -> 0 us
  blocking collectives: 69.3 us -> 24 us
  starting transfers between devices: 28.8 us -> 41.9 us
  local copies, waits for them, and re-layouts: 17 us -> 6.23 us
  Pallas kernels: 0 us -> 9.03 us
  between operations: 23.9 us -> 15 us
  other arithmetic: 13.5 us -> 6.34 us
    unnamed x1 -> x3, waiting for transfers between devices: 0.02 us -> 405 us
    psum x1 -> x0, waiting for transfers between devices: 65.3 us -> none  [on_device(): summed = lax.psum(partial_value.astype(jnp.bfloat16), 'rep')]
    all_to_all x2, waiting for transfers between devices: 85.1 us -> 24.5 us  [the longest x1 24.5 us: on_device(): lax.all_to_all(tiles.reshape(everyone, 2, 128), EVERYONE, split_axis=0, c...]
    all_to_all x3 -> x1, blocking collectives: 69.3 us -> 16.7 us  [on_device(): lax.all_to_all(update, ('zl', 'rep'), split_axis=0, concat_axis=0, tiled=...]
    dot_general x30 -> x0, matrix products: 46.5 us -> none  [the longest x12 12 us: inverse_fourth_root(): image = jnp.dot(statistic, vector, precision=HIGHEST)]
    reduce_sum x15 -> x1, other arithmetic: 10.2 us -> 0.99 us  [pack_statistic(): diagonal = jnp.sum(jnp.where(row == col, last, 0.0), axis=0)]
    pallas_call x0 -> x2, Pallas kernels: none -> 9.03 us  [the longest x1 6.82 us: precondition(): pl.pallas_call(main_kernel, out_shape=jax.ShapeDtypeStruct(pieces.shape[1...]
    all_gather x0 -> x2, blocking collectives: none -> 7.29 us  [the longest x1 4.35 us: on_device(): delivered = lax.all_gather(delivered, 'core')]
  transfers between devices with their start and end apart: 4 -> 7, of which waited for: 3 -> 2; matrix products, arithmetic and copies ran while one was open for 1% -> 1% of each run, Pallas kernels for 0% -> 0%
where the time goes in v1:
time: 532 us
  waiting for transfers between devices  429 us (81%)
  starting transfers between devices  41.9 us (8%)
  blocking collectives  24 us (5%)
  between operations  15 us (3%)
  Pallas kernels  9.03 us (2%)
  other arithmetic  6.34 us (1%)
  local copies, waits for them, and re-layouts  6.23 us (1%)
    unnamed x3, waiting for transfers between devices  405 us
    all_to_all x1, waiting for transfers between devices, on_device(): lax.all_to_all(tiles.reshape(everyone, 2, 128), EVERYONE, split_axis=0, c...  24.5 us
    all_to_all x1, starting transfers between devices, on_device(): lax.all_to_all(tiles.reshape(everyone, 2, 128), EVERYONE, split_axis=0, c...  24.3 us
    all_to_all x1, blocking collectives, on_device(): lax.all_to_all(update, ('zl', 'rep'), split_axis=0, concat_axis=0, tiled=...  16.7 us
  transfers between devices with their start and end apart: 7, of which 2 were waited for; matrix products, arithmetic and copies ran while one was open for 1% of the time, Pallas kernels for 0%

profile of v1, /device:TPU:1, one launch (start us, length us, event | category | flops | bytes accessed | tf_op | source)
XLA Modules:
  0.0 531.6 jit_solution(17646189220444288297)
XLA Ops:
  7.4 0.8 broadcast_multiply_fusion
  8.3 1.0 select_reduce_fusion
  9.5 2.4 broadcast_select_fusion
  12.0 0.8 reshape_squeeze.3
  12.8 1.5 copy.15
  14.4 1.1 fusion
  15.5 0.7 pad_maximum_fusion
  16.2 24.3 %all-to-all-start = ((bf16[512,2,128]{2,1,0:T(2,128)(2,1)}), bf16[512,2,128]{2,1,0:T(2,128)(2,1)S(1)}, u32[]{:S(2)}, u32[]{:S(2)}) async-start(bf16[512,2,128]{2,1,0:T(2,128)(2,1)} %bitcast.5), calls=%async_computation | async-start | bytes 524288 | tf_op jit(solution)/shard_map/all_to_all | solution.py:170
  40.6 0.7 add.79.source_ref
  41.3 24.5 %all-to-all-done.table_ref = bf16[512,2,128]{2,1,0:T(2,128)(2,1)S(1)} async-done(((bf16[512,2,128]{2,1,0:T(2,128)(2,1)}), bf16[512,2,128]{2,1,0:T(2,128)(2,1)S(1)}, u32[]{:S(2)}, u32[]{:S(2)}) %all-to-all-start) | async-done | bytes 262176 | tf_op jit(solution)/shard_map/all_to_all | solution.py:170
  65.8 0.7 copy-done.1
  66.5 2.2 select_rows.1
  68.7 8.5 %all-to-all-start.1 = ((bf16[512,2,128]{2,1,0:T(2,128)(2,1)}), bf16[512,2,128]{2,1,0:T(2,128)(2,1)S(1)}, u32[]{:S(2)}, u32[]{:S(2)}) async-start(bf16[512,2,128]{2,1,0:T(2,128)(2,1)} %select_rows.1), calls=%async_computation.1 | async-start | bytes 524288 | tf_op jit(solution)/shard_map/all_to_all | solution.py:174
  77.3 404.6 %all-reduce.3.cloned.1.call-done = bf16[512,2,256]{2,1,0:T(2,128)(2,1)} async-done(((bf16[512,2,256]{2,1,0:T(2,128)(2,1)}), bf16[512,2,256]{2,1,0:T(2,128)(2,1)}) %all-reduce.3.cloned.1.call-update) | async-done | bytes 524304
  481.9 0.6 dynamic-slice_bitcast_fusion.4.diagonals_ref
  482.6 1.0 dynamic-slice_bitcast_fusion.3
  483.5 1.9 collective-permute-start
  485.4 4.7 collective-permute-start.1
  490.1 2.4 collective-permute-start.2
  492.5 4.4 all_gather.9.packed_ref
  497.0 2.9 all-gather
  499.9 6.8 %precondition.1 = bf16[4,64,512]{2,1,0:T(8,128)(2,1)S(1)} custom-call(s32[2]{0:T(128)S(1)} %pad_add_fusion.place_ref, bf16[2,256,512]{2,1,0:T(8,128)(2,1)S(1)} %all_gather.9.packed_ref, bf16[2,256]{1,0:T(2,128)(2,1)S(1)} %dynamic-slice_bitcast_fusion.4.diagonals_ref, bf16[2,4,64,512]{3,2,1,0:T(8,128)(2,1)S(1)} %bitcast.33), custom_call_target="tpu_custom_call" | custom-call | tf_op jit(solution)/shard_map/precondition/pallas_call | solution.py:130
  506.7 16.7 %all_to_all.15 = bf16[16,16,512]{2,1,0:T(8,128)(2,1)S(1)} all-to-all(bf16[16,16,512]{2,1,0:T(8,128)(2,1)S(1)} %bitcast.34), channel_id=1, replica_groups=mesh['y'=4,'zq'=4,'zl'=4,'core'=2,'rep'=4] {'zl','rep'}, dimensions={0} | all-to-all | bytes 524288 | tf_op jit(solution)/shard_map/all_to_all | solution.py:190
  523.5 0.7 copy.17
  (18 shorter events, 0.5 us)
Async XLA Ops:
  7.4 4.6 copy-start
  7.4 474.5 %all-reduce.3.cloned.1.call-start = ((), (), s32[]{:S(2)}) async-start(), calls=%async_computation.5 | async-start | bytes 1048576
  11.9 470.6 %reduce-scatter.2.cloned.1.call-start = ((), (), s32[]{:S(2)}) async-start(), calls=%async_computation.4 | async-start | bytes 1310720 | tf_op jit(solution)/shard_map/reduce_scatter | solution.py:157
  16.2 49.5 %all-to-all-start = ((bf16[512,2,128]{2,1,0:T(2,128)(2,1)}), bf16[512,2,128]{2,1,0:T(2,128)(2,1)S(1)}, u32[]{:S(2)}, u32[]{:S(2)}) async-start(bf16[512,2,128]{2,1,0:T(2,128)(2,1)} %bitcast.5), calls=%async_computation | async-start | bytes 524288 | tf_op jit(solution)/shard_map/all_to_all | solution.py:170
  65.8 0.7 copy-start.1
  68.7 423.9 %all-to-all-start.1 = ((bf16[512,2,128]{2,1,0:T(2,128)(2,1)}), bf16[512,2,128]{2,1,0:T(2,128)(2,1)S(1)}, u32[]{:S(2)}, u32[]{:S(2)}) async-start(bf16[512,2,128]{2,1,0:T(2,128)(2,1)} %select_rows.1), calls=%async_computation.1 | async-start | bytes 524288 | tf_op jit(solution)/shard_map/all_to_all | solution.py:174
  483.5 13.4 %collective-permute-start = (bf16[64,512]{1,0:T(8,128)(2,1)S(1)}, bf16[64,512]{1,0:T(8,128)(2,1)S(1)}, u32[]{:S(2)}, u32[]{:S(2)}) collective-permute-start(bf16[64,512]{1,0:T(8,128)(2,1)S(1)} %get-tuple-element.10), channel_id=1, source_target_pairs={{0,8},{8,16},{16,24},{24,0},{1,9},{9,17},{17,25},{25,1},{2,10},{10... | collective-permute-start | bytes 196616 | tf_op jit(solution)/shard_map/ppermute | solution.py:182
  485.4 11.5 %collective-permute-start.1 = (bf16[64,512]{1,0:T(8,128)(2,1)S(1)}, bf16[64,512]{1,0:T(8,128)(2,1)S(1)}, u32[]{:S(2)}, u32[]{:S(2)}) collective-permute-start(bf16[64,512]{1,0:T(8,128)(2,1)S(1)} %get-tuple-element.9), channel_id=1, source_target_pairs={{0,16},{8,24},{16,0},{24,8},{1,17},{9,25},{17,1},{25,9},{2,18},{10... | collective-permute-start | bytes 196616 | tf_op jit(solution)/shard_map/ppermute | solution.py:182
  490.1 6.8 %collective-permute-start.2 = (bf16[64,512]{1,0:T(8,128)(2,1)S(1)}, bf16[64,512]{1,0:T(8,128)(2,1)S(1)}, u32[]{:S(2)}, u32[]{:S(2)}) collective-permute-start(bf16[64,512]{1,0:T(8,128)(2,1)S(1)} %get-tuple-element.8), channel_id=1, source_target_pairs={{0,24},{8,0},{16,8},{24,16},{1,25},{9,1},{17,9},{25,17},{2,26},{10... | collective-permute-start | bytes 196616 | tf_op jit(solution)/shard_map/ppermute | solution.py:182
Sparse Core Ops, SparseCore 0:
  13.6 468.2 all-reduce.2
Sparse Core Ops, SparseCore 1:
  15.5 35.4 reduce-scatter.1

commit v2 on v1

v2 whole, which is shorter than its diff:
```python
import jax
import jax.numpy as jnp
from jax import lax
from jax.experimental import pallas as pl
from jax.experimental.pallas import tpu as pltpu
from jax.sharding import Mesh
from jax.sharding import PartitionSpec as P

POWER_STEPS = 6
EPSILON = 1e-06

PLANE = ("y", "zq", "zl", "core")
EVERYONE = PLANE + ("rep",)
CHIP_ROWS = PLANE[:3]
ACROSS = ("core", "rep") + CHIP_ROWS

BF16 = jnp.bfloat16
F32 = jnp.float32


def matmul(a, b, contract=((1,), (0,))):
    return lax.dot_general(a, b, (contract, ((), ())), preferred_element_type=F32)


def grid_of(shape):
    return (
        lax.broadcasted_iota(jnp.int32, shape, 0),
        lax.broadcasted_iota(jnp.int32, shape, 1),
    )


def pack_kernel(stat_ref, packed_ref, diagonal_ref):
    half = packed_ref.shape[0]
    first, last = stat_ref[:half, :half], stat_ref[half:, half:]
    row, col = grid_of((half, half))
    packed_ref[:, :half] = jnp.where(row <= col, first, last).astype(BF16)
    packed_ref[:, half:] = stat_ref[:half, half:].astype(BF16)
    diagonal_ref[...] = jnp.sum(jnp.where(row == col, last, 0.0), axis=0, keepdims=True)


def pack_statistic(stat):
    size = stat.shape[0]
    vmem = pl.BlockSpec(memory_space=pltpu.VMEM)
    return pl.pallas_call(
        pack_kernel,
        out_shape=[
            jax.ShapeDtypeStruct((size // 2, size), BF16),
            jax.ShapeDtypeStruct((1, size // 2), F32),
        ],
        in_specs=[vmem],
        out_specs=[vmem, vmem],
        compiler_params=pltpu.CompilerParams(vmem_limit_bytes=8 * 2**20),
        name="pack_statistic",
    )(stat)


def parts_kernel(place_ref, partial_ref, *parts_refs):
    zl, rep = place_ref[1], place_ref[2]
    zls, rows, size = parts_refs[0].shape
    reps = len(parts_refs)
    for k in range(reps):
        for i in range(zls):
            block = lax.rem(zl + i, zls) * reps + lax.rem(rep + k, reps)
            columns = pl.ds(pl.multiple_of(block * size, size), size)
            parts_refs[k][i] = partial_ref[0, :, columns]


def part_columns(place, partial, reps, zls, size):
    vmem = pl.BlockSpec(memory_space=pltpu.VMEM)
    return pl.pallas_call(
        parts_kernel,
        out_shape=[jax.ShapeDtypeStruct((zls, partial.shape[1], size), BF16)] * reps,
        in_specs=[pl.BlockSpec(memory_space=pltpu.SMEM), vmem],
        out_specs=[vmem] * reps,
        compiler_params=pltpu.CompilerParams(vmem_limit_bytes=8 * 2**20),
        name="part_columns",
    )(place, partial)


def select_kernel(source_ref, table_ref, diagonal_ref, out_ref):
    lines, lanes = table_ref.shape[1:]
    parts = [diagonal_ref[:, line * lanes : (line + 1) * lanes] for line in range(lines)]
    diagonal = jnp.concatenate(parts, axis=0).astype(BF16)
    wide = table_ref.shape[0] // (out_ref.shape[0] - table_ref.shape[0])

    def body(index, carry):
        for j in range(wide):
            out_ref[index * (wide + 1) + j] = table_ref[source_ref[index * wide + j]]
        out_ref[index * (wide + 1) + wide] = diagonal
        return carry

    lax.fori_loop(0, table_ref.shape[0] // wide, body, 0, unroll=64)


def select_rows(source, table, diagonal, wide):
    count, lines, lanes = table.shape
    vmem = pl.BlockSpec(memory_space=pltpu.VMEM)
    return pl.pallas_call(
        select_kernel,
        out_shape=jax.ShapeDtypeStruct((count + count // wide, lines, lanes), table.dtype),
        in_specs=[pl.BlockSpec(memory_space=pltpu.SMEM), vmem, vmem],
        out_specs=vmem,
        compiler_params=pltpu.CompilerParams(vmem_limit_bytes=8 * 2**20),
        name="select_rows",
    )(source, table, diagonal)


def regroup_kernel(place_ref, source_ref, table_ref, out_ref):
    reps, slots, lines, lanes = out_ref.shape
    wide = 2 * reps
    rows = table_ref.shape[0] // (wide + 1)
    plane, row = place_ref[0] * reps + place_ref[2], place_ref[3]

    def body(index, carry):
        for side in range(2):
            for rep in range(reps):
                piece = table_ref[index * (wide + 1) + side * reps + rep]
                out_ref[rep, side * rows + index] = piece
        return carry

    lax.fori_loop(0, rows, body, 0, unroll=4)
    nothing = jnp.zeros((lines, lanes), F32)
    for rep in range(reps):
        for side in range(2):
            origin = source_ref[row * wide + side * reps + rep]
            piece = table_ref[lax.div(origin, wide) * (wide + 1) + wide].astype(F32)
            here = lax.rem(origin, wide) == plane
            out_ref[rep, 2 * rows + side] = jnp.where(here, piece, nothing).astype(BF16)
        for slot in range(2 * rows + 2, slots):
            out_ref[rep, slot] = nothing.astype(BF16)


def regroup(place, source, table, reps, slots):
    smem = pl.BlockSpec(memory_space=pltpu.SMEM)
    vmem = pl.BlockSpec(memory_space=pltpu.VMEM)
    return pl.pallas_call(
        regroup_kernel,
        out_shape=jax.ShapeDtypeStruct((reps, slots) + table.shape[1:], table.dtype),
        in_specs=[smem, smem, vmem],
        out_specs=vmem,
        compiler_params=pltpu.CompilerParams(vmem_limit_bytes=8 * 2**20),
        name="regroup",
    )(place, source, table)


def unfold(packed, diagonal, stat_ref):
    half = packed.shape[0]
    folded = packed[:, :half].astype(F32)
    cross = packed[:, half:].astype(F32)
    row, col = grid_of((half, half))
    turned = folded.T
    stat_ref[:half, :half] += jnp.where(row <= col, folded, turned)
    lower = jnp.where(row > col, folded, turned)
    stat_ref[half:, half:] += jnp.where(row == col, diagonal, lower)
    stat_ref[:half, half:] += cross
    stat_ref[half:, :half] += cross.T


def main_kernel(place_ref, packed_ref, pieces_ref, out_ref, grad_ref, left_ref, right_ref):
    core, zl = place_ref[0], place_ref[1]
    cores, steps, rows, size = pieces_ref.shape
    for step in range(steps):
        origin = lax.rem(zl - step + steps, steps)
        for member in range(cores):
            first = pl.multiple_of((origin * cores + member) * rows, rows)
            grad_ref[pl.ds(first, rows), :] = pieces_ref[member, step]
    gradient = grad_ref[...]
    left_ref[...] = matmul(gradient, gradient, ((1,), (1,)))
    right_ref[...] = matmul(gradient.T, gradient)
    planes = [(member, rep) for member in range(cores) for rep in range(packed_ref.shape[1])]
    part = size // 2 // len(planes)
    diagonals = sum(packed_ref[m, r, 2 * part : 2 * part + 16, :].astype(F32) for m, r in planes)
    for side, ref in enumerate((left_ref, right_ref)):
        packed = [packed_ref[m, r, side * part : (side + 1) * part, :] for m, r in planes]
        lines = [diagonals[2 * side + line : 2 * side + line + 1, : size // 4] for line in range(2)]
        unfold(jnp.concatenate(packed, axis=0), jnp.concatenate(lines, axis=1), ref)
    roots = []
    row, col = grid_of((size, size))
    identity = jnp.where(row == col, 1.0, 0.0)
    images = [jnp.sum(ref[...], axis=0, keepdims=True) for ref in (left_ref, right_ref)]
    for power_step in range(POWER_STEPS):
        axis = 1 - power_step % 2
        scales = [lax.rsqrt(jnp.sum(image * image) + EPSILON) for image in images]
        vectors = images
        images = [
            jnp.sum(ref[...] * vector, axis=axis, keepdims=True) * scale
            for ref, vector, scale in zip((left_ref, right_ref), vectors, scales)
        ]
    vectors = [vector * scale for vector, scale in zip(vectors, scales)]
    for ref, vector, image in zip((left_ref, right_ref), vectors, images):
        turned = jnp.sum(identity * vector, axis=0, keepdims=True)
        largest = jnp.sum(turned * image)
        scaled = ref[...] * (1.0 / largest)
        narrow = scaled.astype(BF16)
        second = matmul(narrow, narrow)
        times = 1.25 * scaled - 0.25 * second
        square = 1.5625 * identity - 0.3125 * scaled - 0.25 * times
        times = times.astype(BF16)
        narrow = square.astype(BF16)
        fourth = matmul(narrow, narrow).astype(BF16)
        last = matmul(fourth, times)
        roots.append((25.0 / 16.0) * identity - (5.0 / 16.0) * scaled - 0.25 * last)
    left, right = roots
    half_way = matmul(left.astype(BF16), gradient)
    raw = matmul(half_way.astype(BF16), right.astype(BF16))
    wide = gradient.astype(F32)
    scale = jnp.sqrt(jnp.sum(wide * wide) + EPSILON) * lax.rsqrt(
        jnp.sum(raw * raw) + EPSILON
    )
    left_ref[...] = raw
    for origin in range(steps):
        first = pl.multiple_of(origin * cores * rows + core * rows, rows)
        out_ref[origin] = (left_ref[pl.ds(first, rows), :] * scale).astype(BF16)


def precondition(place, packed, pieces):
    size = pieces.shape[-1]
    vmem = pl.BlockSpec(memory_space=pltpu.VMEM)
    return pl.pallas_call(
        main_kernel,
        out_shape=jax.ShapeDtypeStruct(pieces.shape[1:], BF16),
        in_specs=[pl.BlockSpec(memory_space=pltpu.SMEM), vmem, vmem],
        out_specs=vmem,
        scratch_shapes=[
            pltpu.VMEM((size, size), BF16),
            pltpu.VMEM((size, size), F32),
            pltpu.VMEM((size, size), F32),
        ],
        compiler_params=pltpu.CompilerParams(vmem_limit_bytes=40 * 2**20),
        name="precondition",
    )(place, packed, pieces)


def on_device(partials, factor_stats, owner_slots):
    rows, width = partials.shape[1:]
    size = factor_stats.shape[-1]
    reps, zls, cores = (lax.axis_size(name) for name in ("rep", "zl", "core"))
    core, zl, rep = (lax.axis_index(name) for name in ("core", "zl", "rep"))
    plane = cores * reps
    place = jnp.stack([core, zl, rep, lax.axis_index(CHIP_ROWS)]).astype(jnp.int32)

    source = 2 * owner_slots.reshape(-1, 1, reps) + jnp.arange(2, dtype=jnp.int32)[None, :, None]
    source = source.reshape(-1)
    everyone = source.shape[0]

    parts = list(part_columns(place, partials, reps, zls, size))
    for step in range(1, reps):
        route = [(index, (index + step) % reps) for index in range(reps)]
        parts[step] = lax.ppermute(parts[step], "rep", route)

    packed, diagonal = pack_statistic(factor_stats[0, 0])
    tiles = packed.reshape(size // 16, 4, 2, size // 128, 128).transpose(0, 3, 1, 2, 4)
    spread = lax.all_to_all(
        tiles.reshape(everyone, 2, 128), ACROSS, split_axis=0, concat_axis=0, tiled=True
    )
    spread, parts = lax.optimization_barrier((spread, parts))
    arrival = source % plane * (everyone // plane) + source // plane
    outgoing = select_rows(arrival, spread, diagonal, plane)
    in_row = lax.all_to_all(outgoing, CHIP_ROWS, split_axis=0, concat_axis=0, tiled=True)

    summed = sum(part.astype(F32) for part in parts).astype(BF16)
    pieces = [summed[0]]
    for step in range(1, zls):
        route = [(index, (index + step) % zls) for index in range(zls)]
        pieces.append(lax.ppermute(summed[step], "zl", route))
    pieces = lax.all_gather(jnp.stack(pieces), "core")
    in_row, pieces = lax.optimization_barrier((in_row, pieces))

    slots = 2 * everyone // plane + 32
    outgoing = regroup(place, source, in_row, reps, slots)
    delivered = lax.all_to_all(outgoing, "rep", split_axis=0, concat_axis=0, tiled=True)
    delivered = delivered.reshape(reps, slots // 16, size // 128, 4, 2, 128)
    delivered = delivered.transpose(0, 1, 3, 4, 2, 5).reshape(reps, slots // 2, size)
    delivered = lax.all_gather(delivered, "core")
    update = precondition(place, delivered, pieces)

    update = update.reshape(zls * reps, rows // reps, size)
    arrived = lax.all_to_all(update, ("zl", "rep"), split_axis=0, concat_axis=0, tiled=True)
    return arrived.transpose(1, 0, 2).reshape(rows // reps, width)


def solution(mesh):
    fsdp, reps = mesh.devices.shape
    fine = Mesh(mesh.devices.reshape(4, 4, fsdp // 32, 2, reps), EVERYONE)
    return jax.shard_map(
        on_device,
        mesh=fine,
        in_specs=(P("rep", PLANE, None), P(PLANE, "rep", None, None), P()),
        out_specs=P(EVERYONE, None),
        check_vma=False,
    )
```

time: 532 us -> 124 us (0.23)
  waiting for transfers between devices: 429 us -> 22.2 us
  between operations: 15 us -> 0.18 us
  starting transfers between devices: 41.9 us -> 55.7 us
  blocking collectives: 24 us -> 32.6 us
  other arithmetic: 6.34 us -> 0.29 us
    unnamed x3 -> x0, waiting for transfers between devices: 405 us -> none
    all_to_all x2, waiting for transfers between devices: 24.5 us -> 4.43 us  [the longest x1 4.43 us: on_device(): lax.all_to_all(tiles.reshape(everyone, 2, 128), ACROSS, split_axis=0, con...]
    ppermute x3 -> x6, waiting for transfers between devices: 0.01 us -> 17.8 us  [the longest x3 9.29 us: on_device(): pieces.append(lax.ppermute(summed[step], 'zl', route))]
    ppermute x3 -> x6, starting transfers between devices: 9 us -> 19.8 us  [the longest x3 10.7 us: on_device(): parts[step] = lax.ppermute(parts[step], 'rep', route)]
    all_to_all x0 -> x1, blocking collectives: none -> 9.66 us  [on_device(): lax.all_to_all(outgoing, 'rep', split_axis=0, concat_axis=0, tiled=True)]
  transfers between devices with their start and end apart: 7 -> 8, of which waited for: 2 -> 4; matrix products, arithmetic and copies ran while one was open for 1% -> 0% of each run, Pallas kernels for 0% -> 1%
where the time goes in v2:
time: 124 us; the launch traced here: 123 us
  starting transfers between devices  55.7 us (45%)
  blocking collectives  32.6 us (26%)
  waiting for transfers between devices  22.2 us (18%)
  Pallas kernels  9.91 us (8%)
  local copies, waits for them, and re-layouts  2.2 us (2%)
    all_to_all x1, starting transfers between devices, on_device(): lax.all_to_all(tiles.reshape(everyone, 2, 128), ACROSS, split_axis=0, con...  24.3 us
    all_to_all x1, blocking collectives, on_device(): lax.all_to_all(update, ('zl', 'rep'), split_axis=0, concat_axis=0, tiled=...  13.8 us
    all_to_all x1, starting transfers between devices, on_device(): lax.all_to_all(outgoing, CHIP_ROWS, split_axis=0, concat_axis=0, tiled=True)  11.7 us
    ppermute x3, starting transfers between devices, on_device(): parts[step] = lax.ppermute(parts[step], 'rep', route)  10.7 us
    all_to_all x1, blocking collectives, on_device(): lax.all_to_all(outgoing, 'rep', split_axis=0, concat_axis=0, tiled=True)  9.66 us
    ppermute x3, waiting for transfers between devices, on_device(): pieces.append(lax.ppermute(summed[step], 'zl', route))  9.29 us
    ppermute x3, starting transfers between devices, on_device(): pieces.append(lax.ppermute(summed[step], 'zl', route))  9.1 us
    ppermute x3, waiting for transfers between devices, on_device(): parts[step] = lax.ppermute(parts[step], 'rep', route)  8.5 us
  transfers between devices with their start and end apart: 8, of which 4 were waited for; matrix products, arithmetic and copies ran while one was open for 0% of the time, Pallas kernels for 1%

profile of v2, /device:TPU:1, one launch (start us, length us, event | category | flops | bytes accessed | tf_op | source)
XLA Modules:
  0.0 123.2 jit_solution(7040842046089319672)
XLA Ops:
  0.0 1.2 copy-done
  1.2 0.7 pack_statistic.1
  2.0 24.3 %all-to-all-start = ((bf16[512,2,128]{2,1,0:T(2,128)(2,1)}), bf16[512,2,128]{2,1,0:T(2,128)(2,1)S(1)}, u32[]{:S(2)}, u32[]{:S(2)}) async-start(bf16[512,2,128]{2,1,0:T(2,128)(2,1)} %bitcast.7), calls=%async_computation | async-start | bytes 524288 | tf_op jit(solution)/shard_map/all_to_all | solution.py:253
  26.4 0.6 part_columns.1
  27.0 3.3 %collective-permute-start = (bf16[4,64,512]{2,1,0:T(8,128)(2,1)S(1)}, bf16[4,64,512]{2,1,0:T(8,128)(2,1)S(1)}, u32[]{:S(2)}, u32[]{:S(2)}) collective-permute-start(bf16[4,64,512]{2,1,0:T(8,128)(2,1)S(1)} %get-tuple-element.20), channel_id=1, source_target_pairs={{0,1},{1,2},{2,3},{3,0},{4,5},{5,6},{6,7},{7,4},{8,9},{9,10},{10,1... | collective-permute-start | bytes 786440 | tf_op jit(solution)/shard_map/ppermute | solution.py:249
  30.3 4.3 %collective-permute-start.1 = (bf16[4,64,512]{2,1,0:T(8,128)(2,1)S(1)}, bf16[4,64,512]{2,1,0:T(8,128)(2,1)S(1)}, u32[]{:S(2)}, u32[]{:S(2)}) collective-permute-start(bf16[4,64,512]{2,1,0:T(8,128)(2,1)S(1)} %get-tuple-element.21), channel_id=1, source_target_pairs={{0,2},{1,3},{2,0},{3,1},{4,6},{5,7},{6,4},{7,5},{8,10},{9,11},{10,... | collective-permute-start | bytes 786440 | tf_op jit(solution)/shard_map/ppermute | solution.py:249
  34.6 3.1 %collective-permute-start.2 = (bf16[4,64,512]{2,1,0:T(8,128)(2,1)S(1)}, bf16[4,64,512]{2,1,0:T(8,128)(2,1)S(1)}, u32[]{:S(2)}, u32[]{:S(2)}) collective-permute-start(bf16[4,64,512]{2,1,0:T(8,128)(2,1)S(1)} %get-tuple-element.22), channel_id=1, source_target_pairs={{0,3},{1,0},{2,1},{3,2},{4,7},{5,4},{6,5},{7,6},{8,11},{9,8},{10,9... | collective-permute-start | bytes 786440 | tf_op jit(solution)/shard_map/ppermute | solution.py:249
  38.1 8.5 %collective-permute-done.1 = bf16[4,64,512]{2,1,0:T(8,128)(2,1)S(1)} collective-permute-done((bf16[4,64,512]{2,1,0:T(8,128)(2,1)S(1)}, bf16[4,64,512]{2,1,0:T(8,128)(2,1)S(1)}, u32[]{:S(2)}, u32[]{:S(2)}) %collective-permute-start.1) | collective-permute-done | bytes 262176 | tf_op jit(solution)/shard_map/ppermute | solution.py:249
  46.6 4.4 %all-to-all-done.table_ref = bf16[512,2,128]{2,1,0:T(2,128)(2,1)S(1)} async-done(((bf16[512,2,128]{2,1,0:T(2,128)(2,1)}), bf16[512,2,128]{2,1,0:T(2,128)(2,1)S(1)}, u32[]{:S(2)}, u32[]{:S(2)}) %all-to-all-start) | async-done | bytes 262176 | tf_op jit(solution)/shard_map/all_to_all | solution.py:253
  51.0 1.5 %select_rows.1 = bf16[576,2,128]{2,1,0:T(2,128)(2,1)} custom-call(s32[512]{0:T(512)S(1)} %fusion.1.source_ref, bf16[512,2,128]{2,1,0:T(2,128)(2,1)S(1)} %all-to-all-done.table_ref, f32[1,256]{1,0:T(1,128)S(1)} %get-tuple-element.24.diagonal_ref), custom_call_target="tpu_custom_call" | custom-call | tf_op jit(solution)/shard_map/select_rows/pallas_call | solution.py:98
  52.5 11.7 %all-to-all-start.1 = ((bf16[576,2,128]{2,1,0:T(2,128)(2,1)}), bf16[576,2,128]{2,1,0:T(2,128)(2,1)S(1)}, u32[]{:S(2)}, u32[]{:S(2)}) async-start(bf16[576,2,128]{2,1,0:T(2,128)(2,1)} %select_rows.1), calls=%async_computation.1 | async-start | bytes 589824 | tf_op jit(solution)/shard_map/all_to_all | solution.py:259
  64.2 0.1 add_convert_fusion
  64.4 3.8 %collective-permute-start.4 = (bf16[64,512]{1,0:T(8,128)(2,1)S(1)}, bf16[64,512]{1,0:T(8,128)(2,1)S(1)}, u32[]{:S(2)}, u32[]{:S(2)}) collective-permute-start(bf16[64,512]{1,0:T(8,128)(2,1)S(1)} %get-tuple-element.33), channel_id=1, source_target_pairs={{0,16},{8,24},{16,0},{24,8},{1,17},{9,25},{17,1},{25,9},{2,18},{10... | collective-permute-start | bytes 196616 | tf_op jit(solution)/shard_map/ppermute | solution.py:265
  68.2 3.1 %collective-permute-start.5 = (bf16[64,512]{1,0:T(8,128)(2,1)S(1)}, bf16[64,512]{1,0:T(8,128)(2,1)S(1)}, u32[]{:S(2)}, u32[]{:S(2)}) collective-permute-start(bf16[64,512]{1,0:T(8,128)(2,1)S(1)} %get-tuple-element.32), channel_id=1, source_target_pairs={{0,24},{8,0},{16,8},{24,16},{1,25},{9,1},{17,9},{25,17},{2,26},{10... | collective-permute-start | bytes 196616 | tf_op jit(solution)/shard_map/ppermute | solution.py:265
  71.3 2.2 %collective-permute-start.3 = (bf16[64,512]{1,0:T(8,128)(2,1)S(1)}, bf16[64,512]{1,0:T(8,128)(2,1)S(1)}, u32[]{:S(2)}, u32[]{:S(2)}) collective-permute-start(bf16[64,512]{1,0:T(8,128)(2,1)S(1)} %get-tuple-element.34), channel_id=1, source_target_pairs={{0,8},{8,16},{16,24},{24,0},{1,9},{9,17},{17,25},{25,1},{2,10},{10... | collective-permute-start | bytes 196616 | tf_op jit(solution)/shard_map/ppermute | solution.py:265
  73.5 4.3 %collective-permute-done.4 = bf16[64,512]{1,0:T(8,128)(2,1)S(1)} collective-permute-done((bf16[64,512]{1,0:T(8,128)(2,1)S(1)}, bf16[64,512]{1,0:T(8,128)(2,1)S(1)}, u32[]{:S(2)}, u32[]{:S(2)}) %collective-permute-start.4) | collective-permute-done | bytes 65568 | tf_op jit(solution)/shard_map/ppermute | solution.py:265
  77.8 5.0 %collective-permute-done.3 = bf16[64,512]{1,0:T(8,128)(2,1)S(1)} collective-permute-done((bf16[64,512]{1,0:T(8,128)(2,1)S(1)}, bf16[64,512]{1,0:T(8,128)(2,1)S(1)}, u32[]{:S(2)}, u32[]{:S(2)}) %collective-permute-start.3) | collective-permute-done | bytes 65568 | tf_op jit(solution)/shard_map/ppermute | solution.py:265
  82.8 4.4 %all-gather = bf16[8,64,512]{2,1,0:T(8,128)(2,1)S(1)} all-gather(bf16[4,64,512]{2,1,0:T(8,128)(2,1)S(1)} %pad_maximum_fusion), channel_id=2, replica_groups=mesh['y'=4,'zq'=4,'zl'=4,'core'=2,'rep'=4] {'core'}, dimensions={0}, use_global_device_ids=true | all-gather | bytes 786432 | tf_op jit(solution)/shard_map/all_gather | solution.py:266
  87.2 0.9 regroup.1
  88.1 9.7 %all_to_all.20 = bf16[4,160,2,128]{3,2,1,0:T(2,128)(2,1)S(1)} all-to-all(bf16[4,160,2,128]{3,2,1,0:T(2,128)(2,1)S(1)} %regroup.1), channel_id=1, replica_groups=mesh['y'=4,'zq'=4,'zl'=4,'core'=2,'rep'=4] {'rep'}, dimensions={0} | all-to-all | bytes 655360 | tf_op jit(solution)/shard_map/all_to_all | solution.py:271
  97.8 4.8 %all_gather.11.packed_ref = bf16[2,4,80,512]{3,2,1,0:T(8,128)(2,1)S(1)} all-gather(bf16[1,4,80,512]{3,2,1,0:T(8,128)(2,1)S(1)} %bitcast.32), channel_id=1, replica_groups=mesh['y'=4,'zq'=4,'zl'=4,'core'=2,'rep'=4] {'core'}, dimensions={0}, use_global_device_ids=true | all-gather | bytes 983040 | tf_op jit(solution)/shard_map/all_gather | solution.py:274
  102.6 6.1 %precondition.1 = bf16[4,64,512]{2,1,0:T(8,128)(2,1)S(1)} custom-call(s32[4]{0:T(128)S(1)} %pad_add_fusion.place_ref, bf16[2,4,80,512]{3,2,1,0:T(8,128)(2,1)S(1)} %all_gather.11.packed_ref, bf16[2,4,64,512]{3,2,1,0:T(8,128)(2,1)S(1)} %bitcast.29), custom_call_target="tpu_custom_call" | custom-call | tf_op jit(solution)/shard_map/precondition/pallas_call | solution.py:219
  108.7 13.8 %all_to_all.21 = bf16[16,16,512]{2,1,0:T(8,128)(2,1)S(1)} all-to-all(bf16[16,16,512]{2,1,0:T(8,128)(2,1)S(1)} %bitcast.31), channel_id=1, replica_groups=mesh['y'=4,'zq'=4,'zl'=4,'core'=2,'rep'=4] {'zl','rep'}, dimensions={0} | all-to-all | bytes 524288 | tf_op jit(solution)/shard_map/all_to_all | solution.py:278
  122.5 0.7 copy.13
  (17 shorter events, 0.4 us)
Async XLA Ops:
  0.0 1.2 copy-start
  1.2 25.2 %copy-start.1 = (bf16[1,64,8192]{2,1,0:T(8,128)(2,1)S(1)}, bf16[1,64,8192]{2,1,0:T(8,128)(2,1)}, u32[]{:S(2)}) copy-start(bf16[1,64,8192]{2,1,0:T(8,128)(2,1)} %partial_ref.1) | copy-start | bytes 3145732
  2.0 49.0 %all-to-all-start = ((bf16[512,2,128]{2,1,0:T(2,128)(2,1)}), bf16[512,2,128]{2,1,0:T(2,128)(2,1)S(1)}, u32[]{:S(2)}, u32[]{:S(2)}) async-start(bf16[512,2,128]{2,1,0:T(2,128)(2,1)} %bitcast.7), calls=%async_computation | async-start | bytes 524288 | tf_op jit(solution)/shard_map/all_to_all | solution.py:253
  27.0 11.0 %collective-permute-start = (bf16[4,64,512]{2,1,0:T(8,128)(2,1)S(1)}, bf16[4,64,512]{2,1,0:T(8,128)(2,1)S(1)}, u32[]{:S(2)}, u32[]{:S(2)}) collective-permute-start(bf16[4,64,512]{2,1,0:T(8,128)(2,1)S(1)} %get-tuple-element.20), channel_id=1, source_target_pairs={{0,1},{1,2},{2,3},{3,0},{4,5},{5,6},{6,7},{7,4},{8,9},{9,10},{10,1... | collective-permute-start | bytes 786440 | tf_op jit(solution)/shard_map/ppermute | solution.py:249
  30.3 7.4 %copy-start.2 = (s32[256]{0:T(256)S(1)}, s32[256]{0:T(256)}, u32[]{:S(2)}) copy-start(s32[256]{0:T(256)} %param.5) | copy-start | bytes 3076
  30.3 16.2 %collective-permute-start.1 = (bf16[4,64,512]{2,1,0:T(8,128)(2,1)S(1)}, bf16[4,64,512]{2,1,0:T(8,128)(2,1)S(1)}, u32[]{:S(2)}, u32[]{:S(2)}) collective-permute-start(bf16[4,64,512]{2,1,0:T(8,128)(2,1)S(1)} %get-tuple-element.21), channel_id=1, source_target_pairs={{0,2},{1,3},{2,0},{3,1},{4,6},{5,7},{6,4},{7,5},{8,10},{9,11},{10,... | collective-permute-start | bytes 786440 | tf_op jit(solution)/shard_map/ppermute | solution.py:249
  34.6 11.9 %collective-permute-start.2 = (bf16[4,64,512]{2,1,0:T(8,128)(2,1)S(1)}, bf16[4,64,512]{2,1,0:T(8,128)(2,1)S(1)}, u32[]{:S(2)}, u32[]{:S(2)}) collective-permute-start(bf16[4,64,512]{2,1,0:T(8,128)(2,1)S(1)} %get-tuple-element.22), channel_id=1, source_target_pairs={{0,3},{1,0},{2,1},{3,2},{4,7},{5,4},{6,5},{7,6},{8,11},{9,8},{10,9... | collective-permute-start | bytes 786440 | tf_op jit(solution)/shard_map/ppermute | solution.py:249
  52.5 34.7 %all-to-all-start.1 = ((bf16[576,2,128]{2,1,0:T(2,128)(2,1)}), bf16[576,2,128]{2,1,0:T(2,128)(2,1)S(1)}, u32[]{:S(2)}, u32[]{:S(2)}) async-start(bf16[576,2,128]{2,1,0:T(2,128)(2,1)} %select_rows.1), calls=%async_computation.1 | async-start | bytes 589824 | tf_op jit(solution)/shard_map/all_to_all | solution.py:259
  64.4 13.4 %collective-permute-start.4 = (bf16[64,512]{1,0:T(8,128)(2,1)S(1)}, bf16[64,512]{1,0:T(8,128)(2,1)S(1)}, u32[]{:S(2)}, u32[]{:S(2)}) collective-permute-start(bf16[64,512]{1,0:T(8,128)(2,1)S(1)} %get-tuple-element.33), channel_id=1, source_target_pairs={{0,16},{8,24},{16,0},{24,8},{1,17},{9,25},{17,1},{25,9},{2,18},{10... | collective-permute-start | bytes 196616 | tf_op jit(solution)/shard_map/ppermute | solution.py:265
  68.2 9.6 %collective-permute-start.5 = (bf16[64,512]{1,0:T(8,128)(2,1)S(1)}, bf16[64,512]{1,0:T(8,128)(2,1)S(1)}, u32[]{:S(2)}, u32[]{:S(2)}) collective-permute-start(bf16[64,512]{1,0:T(8,128)(2,1)S(1)} %get-tuple-element.32), channel_id=1, source_target_pairs={{0,24},{8,0},{16,8},{24,16},{1,25},{9,1},{17,9},{25,17},{2,26},{10... | collective-permute-start | bytes 196616 | tf_op jit(solution)/shard_map/ppermute | solution.py:265
  71.3 11.5 %collective-permute-start.3 = (bf16[64,512]{1,0:T(8,128)(2,1)S(1)}, bf16[64,512]{1,0:T(8,128)(2,1)S(1)}, u32[]{:S(2)}, u32[]{:S(2)}) collective-permute-start(bf16[64,512]{1,0:T(8,128)(2,1)S(1)} %get-tuple-element.34), channel_id=1, source_target_pairs={{0,8},{8,16},{16,24},{24,0},{1,9},{9,17},{17,25},{25,1},{2,10},{10... | collective-permute-start | bytes 196616 | tf_op jit(solution)/shard_map/ppermute | solution.py:265

commit v3 on v2

--- a/solution.py
+++ b/solution.py
@@ -253,7 +253,7 @@
     spread = lax.all_to_all(
         tiles.reshape(everyone, 2, 128), ACROSS, split_axis=0, concat_axis=0, tiled=True
     )
-    spread, parts = lax.optimization_barrier((spread, parts))
+    spread, parts[1], parts[3] = lax.optimization_barrier((spread, parts[1], parts[3]))
     arrival = source % plane * (everyone // plane) + source // plane
     outgoing = select_rows(arrival, spread, diagonal, plane)
     in_row = lax.all_to_all(outgoing, CHIP_ROWS, split_axis=0, concat_axis=0, tiled=True)
@@ -263,8 +263,8 @@
     for step in range(1, zls):
         route = [(index, (index + step) % zls) for index in range(zls)]
         pieces.append(lax.ppermute(summed[step], "zl", route))
+    in_row, pieces[1] = lax.optimization_barrier((in_row, pieces[1]))
     pieces = lax.all_gather(jnp.stack(pieces), "core")
-    in_row, pieces = lax.optimization_barrier((in_row, pieces))
 
     slots = 2 * everyone // plane + 32
     outgoing = regroup(place, source, in_row, reps, slots)

time: 124 us -> 116 us (0.935)
  blocking collectives: 32.6 us -> 25.7 us
  starting transfers between devices: 55.7 us -> 54.2 us
    all_to_all x1 -> x0, blocking collectives: 9.66 us -> none  [on_device(): lax.all_to_all(outgoing, 'rep', split_axis=0, concat_axis=0, tiled=True)]
    ppermute x3, waiting for transfers between devices: 9.29 us -> 0.01 us  [on_device(): pieces.append(lax.ppermute(summed[step], 'zl', route))]
    all_to_all x1, waiting for transfers between devices: 4.43 us -> 12.4 us  [on_device(): lax.all_to_all(tiles.reshape(everyone, 2, 128), ACROSS, split_axis=0, con...]
    all_to_all x1, starting transfers between devices: 11.7 us -> 5.57 us  [on_device(): lax.all_to_all(outgoing, CHIP_ROWS, split_axis=0, concat_axis=0, tiled=True)]
    all_to_all x0 -> x1, starting transfers between devices: none -> 3.81 us  [on_device(): lax.all_to_all(outgoing, 'rep', split_axis=0, concat_axis=0, tiled=True)]
    all_gather x1, blocking collectives: 4.78 us -> 7.05 us  [on_device(): delivered = lax.all_gather(delivered, 'core')]
    all_gather x1, blocking collectives: 4.42 us -> 5.94 us  [on_device(): pieces = lax.all_gather(jnp.stack(pieces), 'core')]
    ppermute x3, waiting for transfers between devices: 8.5 us -> 9.93 us  [on_device(): parts[step] = lax.ppermute(parts[step], 'rep', route)]
  transfers between devices with their start and end apart: 8 -> 9, of which waited for: 4 -> 5; matrix products, arithmetic and copies ran while one was open for 0% -> 0% of each run, Pallas kernels for 1% -> 2%
where the time goes in v3:
time: 116 us
  starting transfers between devices  54.2 us (47%)
  blocking collectives  25.7 us (22%)
  waiting for transfers between devices  22.5 us (19%)
  Pallas kernels  10.6 us (9%)
  local copies, waits for them, and re-layouts  2.2 us (2%)
    all_to_all x1, starting transfers between devices, on_device(): lax.all_to_all(tiles.reshape(everyone, 2, 128), ACROSS, split_axis=0, con...  24.3 us
    all_to_all x1, blocking collectives, on_device(): lax.all_to_all(update, ('zl', 'rep'), split_axis=0, concat_axis=0, tiled=...  12.7 us
    all_to_all x1, waiting for transfers between devices, on_device(): lax.all_to_all(tiles.reshape(everyone, 2, 128), ACROSS, split_axis=0, con...  12.4 us
    ppermute x3, starting transfers between devices, on_device(): parts[step] = lax.ppermute(parts[step], 'rep', route)  10.8 us
    ppermute x3, waiting for transfers between devices, on_device(): parts[step] = lax.ppermute(parts[step], 'rep', route)  9.93 us
    ppermute x3, starting transfers between devices, on_device(): pieces.append(lax.ppermute(summed[step], 'zl', route))  9.72 us
    all_gather x1, blocking collectives, on_device(): delivered = lax.all_gather(delivered, 'core')  7.05 us
    pallas_call x1, Pallas kernels, precondition(): pl.pallas_call(main_kernel, out_shape=jax.ShapeDtypeStruct(pieces.shape[1...  6.12 us
  transfers between devices with their start and end apart: 9, of which 5 were waited for; matrix products, arithmetic and copies ran while one was open for 0% of the time, Pallas kernels for 2%

profile of v3, /device:TPU:1, one launch (start us, length us, event | category | flops | bytes accessed | tf_op | source)
XLA Modules:
  0.0 115.7 jit_solution(11759362940713376511)
XLA Ops:
  0.0 1.2 %copy-done = f32[1,1,512,512]{3,2,1,0:T(8,128)S(1)} copy-done((f32[1,1,512,512]{3,2,1,0:T(8,128)S(1)}, f32[1,1,512,512]{3,2,1,0:T(8,128)}, u32[]{:S(2)}) %copy-start) | copy-done | bytes 1048600
  1.2 0.7 pack_statistic.1
  2.0 24.3 %all-to-all-start = ((bf16[512,2,128]{2,1,0:T(2,128)(2,1)}), bf16[512,2,128]{2,1,0:T(2,128)(2,1)S(1)}, u32[]{:S(2)}, u32[]{:S(2)}) async-start(bf16[512,2,128]{2,1,0:T(2,128)(2,1)} %bitcast.7), calls=%async_computation | async-start | bytes 524288 | tf_op jit(solution)/shard_map/all_to_all | solution.py:253
  26.4 0.6 part_columns.1
  27.0 3.3 %collective-permute-start = (bf16[4,64,512]{2,1,0:T(8,128)(2,1)S(1)}, bf16[4,64,512]{2,1,0:T(8,128)(2,1)S(1)}, u32[]{:S(2)}, u32[]{:S(2)}) collective-permute-start(bf16[4,64,512]{2,1,0:T(8,128)(2,1)S(1)} %get-tuple-element.17), channel_id=1, source_target_pairs={{0,1},{1,2},{2,3},{3,0},{4,5},{5,6},{6,7},{7,4},{8,9},{9,10},{10,1... | collective-permute-start | bytes 786440 | tf_op jit(solution)/shard_map/ppermute | solution.py:249
  30.3 3.2 %collective-permute-start.1 = (bf16[4,64,512]{2,1,0:T(8,128)(2,1)S(1)}, bf16[4,64,512]{2,1,0:T(8,128)(2,1)S(1)}, u32[]{:S(2)}, u32[]{:S(2)}) collective-permute-start(bf16[4,64,512]{2,1,0:T(8,128)(2,1)S(1)} %get-tuple-element.18), channel_id=1, source_target_pairs={{0,3},{1,0},{2,1},{3,2},{4,7},{5,4},{6,5},{7,6},{8,11},{9,8},{10,9... | collective-permute-start | bytes 786440 | tf_op jit(solution)/shard_map/ppermute | solution.py:249
  33.8 2.5 %collective-permute-done = bf16[4,64,512]{2,1,0:T(8,128)(2,1)S(1)} collective-permute-done((bf16[4,64,512]{2,1,0:T(8,128)(2,1)S(1)}, bf16[4,64,512]{2,1,0:T(8,128)(2,1)S(1)}, u32[]{:S(2)}, u32[]{:S(2)}) %collective-permute-start) | collective-permute-done | bytes 262176 | tf_op jit(solution)/shard_map/ppermute | solution.py:249
  36.3 2.2 %collective-permute-done.1 = bf16[4,64,512]{2,1,0:T(8,128)(2,1)S(1)} collective-permute-done((bf16[4,64,512]{2,1,0:T(8,128)(2,1)S(1)}, bf16[4,64,512]{2,1,0:T(8,128)(2,1)S(1)}, u32[]{:S(2)}, u32[]{:S(2)}) %collective-permute-start.1) | collective-permute-done | bytes 262176 | tf_op jit(solution)/shard_map/ppermute | solution.py:249
  38.6 12.4 %all-to-all-done.table_ref = bf16[512,2,128]{2,1,0:T(2,128)(2,1)S(1)} async-done(((bf16[512,2,128]{2,1,0:T(2,128)(2,1)}), bf16[512,2,128]{2,1,0:T(2,128)(2,1)S(1)}, u32[]{:S(2)}, u32[]{:S(2)}) %all-to-all-start) | async-done | bytes 262176 | tf_op jit(solution)/shard_map/all_to_all | solution.py:253
  51.0 1.6 %select_rows.1 = bf16[576,2,128]{2,1,0:T(2,128)(2,1)} custom-call(s32[512]{0:T(512)S(1)} %fusion.1.source_ref, bf16[512,2,128]{2,1,0:T(2,128)(2,1)S(1)} %all-to-all-done.table_ref, f32[1,256]{1,0:T(1,128)S(1)} %get-tuple-element.20.diagonal_ref), custom_call_target="tpu_custom_call" | custom-call | tf_op jit(solution)/shard_map/select_rows/pallas_call | solution.py:98
  52.5 5.6 %all-to-all-start.1 = ((bf16[576,2,128]{2,1,0:T(2,128)(2,1)}), bf16[576,2,128]{2,1,0:T(2,128)(2,1)S(1)}, u32[]{:S(2)}, u32[]{:S(2)}) async-start(bf16[576,2,128]{2,1,0:T(2,128)(2,1)} %select_rows.1), calls=%async_computation.1 | async-start | bytes 589824 | tf_op jit(solution)/shard_map/all_to_all | solution.py:259
  58.1 4.3 %collective-permute-start.2 = (bf16[4,64,512]{2,1,0:T(8,128)(2,1)S(1)}, bf16[4,64,512]{2,1,0:T(8,128)(2,1)S(1)}, u32[]{:S(2)}, u32[]{:S(2)}) collective-permute-start(bf16[4,64,512]{2,1,0:T(8,128)(2,1)S(1)} %get-tuple-element.23), channel_id=1, source_target_pairs={{0,2},{1,3},{2,0},{3,1},{4,6},{5,7},{6,4},{7,5},{8,10},{9,11},{10,... | collective-permute-start | bytes 786440 | tf_op jit(solution)/shard_map/ppermute | solution.py:249
  62.5 5.2 %collective-permute-done.2 = bf16[4,64,512]{2,1,0:T(8,128)(2,1)S(1)} collective-permute-done((bf16[4,64,512]{2,1,0:T(8,128)(2,1)S(1)}, bf16[4,64,512]{2,1,0:T(8,128)(2,1)S(1)}, u32[]{:S(2)}, u32[]{:S(2)}) %collective-permute-start.2) | collective-permute-done | bytes 262176 | tf_op jit(solution)/shard_map/ppermute | solution.py:249
  67.8 2.6 %collective-permute-start.3 = (bf16[64,512]{1,0:T(8,128)(2,1)S(1)}, bf16[64,512]{1,0:T(8,128)(2,1)S(1)}, u32[]{:S(2)}, u32[]{:S(2)}) collective-permute-start(bf16[64,512]{1,0:T(8,128)(2,1)S(1)} %get-tuple-element.30), channel_id=1, source_target_pairs={{0,8},{8,16},{16,24},{24,0},{1,9},{9,17},{17,25},{25,1},{2,10},{10... | collective-permute-start | bytes 196616 | tf_op jit(solution)/shard_map/ppermute | solution.py:265
  70.5 4.0 %collective-permute-start.4 = (bf16[64,512]{1,0:T(8,128)(2,1)S(1)}, bf16[64,512]{1,0:T(8,128)(2,1)S(1)}, u32[]{:S(2)}, u32[]{:S(2)}) collective-permute-start(bf16[64,512]{1,0:T(8,128)(2,1)S(1)} %get-tuple-element.29), channel_id=1, source_target_pairs={{0,16},{8,24},{16,0},{24,8},{1,17},{9,25},{17,1},{25,9},{2,18},{10... | collective-permute-start | bytes 196616 | tf_op jit(solution)/shard_map/ppermute | solution.py:265
  74.5 3.1 %collective-permute-start.5 = (bf16[64,512]{1,0:T(8,128)(2,1)S(1)}, bf16[64,512]{1,0:T(8,128)(2,1)S(1)}, u32[]{:S(2)}, u32[]{:S(2)}) collective-permute-start(bf16[64,512]{1,0:T(8,128)(2,1)S(1)} %get-tuple-element.28), channel_id=1, source_target_pairs={{0,24},{8,0},{16,8},{24,16},{1,25},{9,1},{17,9},{25,17},{2,26},{10... | collective-permute-start | bytes 196616 | tf_op jit(solution)/shard_map/ppermute | solution.py:265
  77.6 0.1 all-to-all-done.1.table_ref
  77.7 1.6 %regroup.1 = bf16[4,160,2,128]{3,2,1,0:T(2,128)(2,1)} custom-call(s32[4]{0:T(128)S(1)} %pad_add_fusion.place_ref, s32[512]{0:T(512)S(1)} %add.47.source_ref, bf16[576,2,128]{2,1,0:T(2,128)(2,1)S(1)} %all-to-all-done.1.table_ref), custom_call_target="tpu_custom_call" | custom-call | tf_op jit(solution)/shard_map/regroup/pallas_call | solution.py:136
  79.3 3.8 %all-to-all-start.2 = ((bf16[4,160,2,128]{3,2,1,0:T(2,128)(2,1)}), bf16[4,160,2,128]{3,2,1,0:T(2,128)(2,1)S(1)}, u32[]{:S(2)}, u32[]{:S(2)}) async-start(bf16[4,160,2,128]{3,2,1,0:T(2,128)(2,1)} %regroup.1), calls=%async_computation.2 | async-start | bytes 655360 | tf_op jit(solution)/shard_map/all_to_all | solution.py:271
  83.2 5.9 %all-gather = bf16[8,64,512]{2,1,0:T(8,128)(2,1)S(1)} all-gather(bf16[4,64,512]{2,1,0:T(8,128)(2,1)S(1)} %pad_maximum_fusion), channel_id=2, replica_groups=mesh['y'=4,'zq'=4,'zl'=4,'core'=2,'rep'=4] {'core'}, dimensions={0}, use_global_device_ids=true | all-gather | bytes 786432 | tf_op jit(solution)/shard_map/all_gather | solution.py:267
  89.2 7.1 %all_gather.9.packed_ref = bf16[2,4,80,512]{3,2,1,0:T(8,128)(2,1)S(1)} all-gather(bf16[1,4,80,512]{3,2,1,0:T(8,128)(2,1)S(1)} %bitcast.32), channel_id=1, replica_groups=mesh['y'=4,'zq'=4,'zl'=4,'core'=2,'rep'=4] {'core'}, dimensions={0}, use_global_device_ids=true | all-gather | bytes 983040 | tf_op jit(solution)/shard_map/all_gather | solution.py:274
  96.2 6.1 %precondition.1 = bf16[4,64,512]{2,1,0:T(8,128)(2,1)S(1)} custom-call(s32[4]{0:T(128)S(1)} %pad_add_fusion.place_ref, bf16[2,4,80,512]{3,2,1,0:T(8,128)(2,1)S(1)} %all_gather.9.packed_ref, bf16[2,4,64,512]{3,2,1,0:T(8,128)(2,1)S(1)} %bitcast.29), custom_call_target="tpu_custom_call" | custom-call | tf_op jit(solution)/shard_map/precondition/pallas_call | solution.py:219
  102.3 12.7 %all_to_all.20 = bf16[16,16,512]{2,1,0:T(8,128)(2,1)S(1)} all-to-all(bf16[16,16,512]{2,1,0:T(8,128)(2,1)S(1)} %bitcast.31), channel_id=1, replica_groups=mesh['y'=4,'zq'=4,'zl'=4,'core'=2,'rep'=4] {'zl','rep'}, dimensions={0} | all-to-all | bytes 524288 | tf_op jit(solution)/shard_map/all_to_all | solution.py:278
  115.0 0.7 copy.13
  (18 shorter events, 0.6 us)
Async XLA Ops:
  0.0 1.2 %copy-start = (f32[1,1,512,512]{3,2,1,0:T(8,128)S(1)}, f32[1,1,512,512]{3,2,1,0:T(8,128)}, u32[]{:S(2)}) copy-start(f32[1,1,512,512]{3,2,1,0:T(8,128)} %param.4) | copy-start | bytes 3145732
  1.2 25.2 %copy-start.1 = (bf16[1,64,8192]{2,1,0:T(8,128)(2,1)S(1)}, bf16[1,64,8192]{2,1,0:T(8,128)(2,1)}, u32[]{:S(2)}) copy-start(bf16[1,64,8192]{2,1,0:T(8,128)(2,1)} %partial_ref.1) | copy-start | bytes 3145732
  2.0 49.0 %all-to-all-start = ((bf16[512,2,128]{2,1,0:T(2,128)(2,1)}), bf16[512,2,128]{2,1,0:T(2,128)(2,1)S(1)}, u32[]{:S(2)}, u32[]{:S(2)}) async-start(bf16[512,2,128]{2,1,0:T(2,128)(2,1)} %bitcast.7), calls=%async_computation | async-start | bytes 524288 | tf_op jit(solution)/shard_map/all_to_all | solution.py:253
  27.0 6.5 %copy-start.2 = (s32[256]{0:T(256)S(1)}, s32[256]{0:T(256)}, u32[]{:S(2)}) copy-start(s32[256]{0:T(256)} %param.5) | copy-start | bytes 3076
  27.0 9.3 %collective-permute-start = (bf16[4,64,512]{2,1,0:T(8,128)(2,1)S(1)}, bf16[4,64,512]{2,1,0:T(8,128)(2,1)S(1)}, u32[]{:S(2)}, u32[]{:S(2)}) collective-permute-start(bf16[4,64,512]{2,1,0:T(8,128)(2,1)S(1)} %get-tuple-element.17), channel_id=1, source_target_pairs={{0,1},{1,2},{2,3},{3,0},{4,5},{5,6},{6,7},{7,4},{8,9},{9,10},{10,1... | collective-permute-start | bytes 786440 | tf_op jit(solution)/shard_map/ppermute | solution.py:249
  30.3 8.2 %collective-permute-start.1 = (bf16[4,64,512]{2,1,0:T(8,128)(2,1)S(1)}, bf16[4,64,512]{2,1,0:T(8,128)(2,1)S(1)}, u32[]{:S(2)}, u32[]{:S(2)}) collective-permute-start(bf16[4,64,512]{2,1,0:T(8,128)(2,1)S(1)} %get-tuple-element.18), channel_id=1, source_target_pairs={{0,3},{1,0},{2,1},{3,2},{4,7},{5,4},{6,5},{7,6},{8,11},{9,8},{10,9... | collective-permute-start | bytes 786440 | tf_op jit(solution)/shard_map/ppermute | solution.py:249
  52.5 25.2 %all-to-all-start.1 = ((bf16[576,2,128]{2,1,0:T(2,128)(2,1)}), bf16[576,2,128]{2,1,0:T(2,128)(2,1)S(1)}, u32[]{:S(2)}, u32[]{:S(2)}) async-start(bf16[576,2,128]{2,1,0:T(2,128)(2,1)} %select_rows.1), calls=%async_computation.1 | async-start | bytes 589824 | tf_op jit(solution)/shard_map/all_to_all | solution.py:259
  58.1 9.6 %collective-permute-start.2 = (bf16[4,64,512]{2,1,0:T(8,128)(2,1)S(1)}, bf16[4,64,512]{2,1,0:T(8,128)(2,1)S(1)}, u32[]{:S(2)}, u32[]{:S(2)}) collective-permute-start(bf16[4,64,512]{2,1,0:T(8,128)(2,1)S(1)} %get-tuple-element.23), channel_id=1, source_target_pairs={{0,2},{1,3},{2,0},{3,1},{4,6},{5,7},{6,4},{7,5},{8,10},{9,11},{10,... | collective-permute-start | bytes 786440 | tf_op jit(solution)/shard_map/ppermute | solution.py:249
  67.8 9.7 %collective-permute-start.3 = (bf16[64,512]{1,0:T(8,128)(2,1)S(1)}, bf16[64,512]{1,0:T(8,128)(2,1)S(1)}, u32[]{:S(2)}, u32[]{:S(2)}) collective-permute-start(bf16[64,512]{1,0:T(8,128)(2,1)S(1)} %get-tuple-element.30), channel_id=1, source_target_pairs={{0,8},{8,16},{16,24},{24,0},{1,9},{9,17},{17,25},{25,1},{2,10},{10... | collective-permute-start | bytes 196616 | tf_op jit(solution)/shard_map/ppermute | solution.py:265
  70.5 12.7 %collective-permute-start.4 = (bf16[64,512]{1,0:T(8,128)(2,1)S(1)}, bf16[64,512]{1,0:T(8,128)(2,1)S(1)}, u32[]{:S(2)}, u32[]{:S(2)}) collective-permute-start(bf16[64,512]{1,0:T(8,128)(2,1)S(1)} %get-tuple-element.29), channel_id=1, source_target_pairs={{0,16},{8,24},{16,0},{24,8},{1,17},{9,25},{17,1},{25,9},{2,18},{10... | collective-permute-start | bytes 196616 | tf_op jit(solution)/shard_map/ppermute | solution.py:265
  74.5 8.7 %collective-permute-start.5 = (bf16[64,512]{1,0:T(8,128)(2,1)S(1)}, bf16[64,512]{1,0:T(8,128)(2,1)S(1)}, u32[]{:S(2)}, u32[]{:S(2)}) collective-permute-start(bf16[64,512]{1,0:T(8,128)(2,1)S(1)} %get-tuple-element.28), channel_id=1, source_target_pairs={{0,24},{8,0},{16,8},{24,16},{1,25},{9,1},{17,9},{25,17},{2,26},{10... | collective-permute-start | bytes 196616 | tf_op jit(solution)/shard_map/ppermute | solution.py:265
  79.3 9.8 %all-to-all-start.2 = ((bf16[4,160,2,128]{3,2,1,0:T(2,128)(2,1)}), bf16[4,160,2,128]{3,2,1,0:T(2,128)(2,1)S(1)}, u32[]{:S(2)}, u32[]{:S(2)}) async-start(bf16[4,160,2,128]{3,2,1,0:T(2,128)(2,1)} %regroup.1), calls=%async_computation.2 | async-start | bytes 655360 | tf_op jit(solution)/shard_map/all_to_all | solution.py:271

commit v4 on v3

--- a/solution.py
+++ b/solution.py
@@ -169,12 +169,11 @@
     right_ref[...] = matmul(gradient.T, gradient)
     planes = [(member, rep) for member in range(cores) for rep in range(packed_ref.shape[1])]
     part = size // 2 // len(planes)
-    diagonals = sum(packed_ref[m, r, 2 * part : 2 * part + 16, :].astype(F32) for m, r in planes)
+    diagonals = sum(packed_ref[m, r].astype(F32)[2 * part :, : size // 4] for m, r in planes)
     for side, ref in enumerate((left_ref, right_ref)):
         packed = [packed_ref[m, r, side * part : (side + 1) * part, :] for m, r in planes]
-        lines = [diagonals[2 * side + line : 2 * side + line + 1, : size // 4] for line in range(2)]
+        lines = [diagonals[2 * side + line : 2 * side + line + 1, :] for line in range(2)]
         unfold(jnp.concatenate(packed, axis=0), jnp.concatenate(lines, axis=1), ref)
-    roots = []
     row, col = grid_of((size, size))
     identity = jnp.where(row == col, 1.0, 0.0)
     images = [jnp.sum(ref[...], axis=0, keepdims=True) for ref in (left_ref, right_ref)]
@@ -187,19 +186,21 @@
             for ref, vector, scale in zip((left_ref, right_ref), vectors, scales)
         ]
     vectors = [vector * scale for vector, scale in zip(vectors, scales)]
+    scaleds = []
     for ref, vector, image in zip((left_ref, right_ref), vectors, images):
         turned = jnp.sum(identity * vector, axis=0, keepdims=True)
-        largest = jnp.sum(turned * image)
-        scaled = ref[...] * (1.0 / largest)
-        narrow = scaled.astype(BF16)
-        second = matmul(narrow, narrow)
-        times = 1.25 * scaled - 0.25 * second
-        square = 1.5625 * identity - 0.3125 * scaled - 0.25 * times
-        times = times.astype(BF16)
-        narrow = square.astype(BF16)
-        fourth = matmul(narrow, narrow).astype(BF16)
-        last = matmul(fourth, times)
-        roots.append((25.0 / 16.0) * identity - (5.0 / 16.0) * scaled - 0.25 * last)
+        scaleds.append(ref[...] * (1.0 / jnp.sum(turned * image)))
+    narrows = [scaled.astype(BF16) for scaled in scaleds]
+    times = [1.25 * scaled - 0.25 * matmul(n, n) for scaled, n in zip(scaleds, narrows)]
+    squares = [
+        (1.5625 * identity - 0.3125 * scaled - 0.25 * t).astype(BF16)
+        for scaled, t in zip(scaleds, times)
+    ]
+    fourths = [matmul(square, square).astype(BF16) for square in squares]
+    lasts = [matmul(fourth, t.astype(BF16)) for fourth, t in zip(fourths, times)]
+    roots = [
+        1.5625 * identity - 0.3125 * scaled - 0.25 * last for scaled, last in zip(scaleds, lasts)
+    ]
     left, right = roots
     half_way = matmul(left.astype(BF16), gradient)
     raw = matmul(half_way.astype(BF16), right.astype(BF16))
@@ -266,7 +267,7 @@
     in_row, pieces[1] = lax.optimization_barrier((in_row, pieces[1]))
     pieces = lax.all_gather(jnp.stack(pieces), "core")
 
-    slots = 2 * everyone // plane + 32
+    slots = 2 * everyone // plane + 16
     outgoing = regroup(place, source, in_row, reps, slots)
     delivered = lax.all_to_all(outgoing, "rep", split_axis=0, concat_axis=0, tiled=True)
     delivered = delivered.reshape(reps, slots // 16, size // 128, 4, 2, 128)

time: 116 us -> 116 us (level)
  no operation moved by 1% of the time
where the time goes in v4:
time: 116 us; the launch traced here: 115 us
  starting transfers between devices  54.2 us (47%)
  blocking collectives  25.4 us (22%)
  waiting for transfers between devices  22.5 us (19%)
  Pallas kernels  10.6 us (9%)
  local copies, waits for them, and re-layouts  2.2 us (2%)
    all_to_all x1, starting transfers between devices, on_device(): lax.all_to_all(tiles.reshape(everyone, 2, 128), ACROSS, split_axis=0, con...  24.3 us
    all_to_all x1, blocking collectives, on_device(): lax.all_to_all(update, ('zl', 'rep'), split_axis=0, concat_axis=0, tiled=...  12.7 us
    all_to_all x1, waiting for transfers between devices, on_device(): lax.all_to_all(tiles.reshape(everyone, 2, 128), ACROSS, split_axis=0, con...  12.4 us
    ppermute x3, starting transfers between devices, on_device(): parts[step] = lax.ppermute(parts[step], 'rep', route)  10.8 us
    ppermute x3, waiting for transfers between devices, on_device(): parts[step] = lax.ppermute(parts[step], 'rep', route)  9.93 us
    ppermute x3, starting transfers between devices, on_device(): pieces.append(lax.ppermute(summed[step], 'zl', route))  9.72 us
    all_gather x1, blocking collectives, on_device(): delivered = lax.all_gather(delivered, 'core')  6.83 us
    pallas_call x1, Pallas kernels, precondition(): pl.pallas_call(main_kernel, out_shape=jax.ShapeDtypeStruct(pieces.shape[1...  6.05 us
  transfers between devices with their start and end apart: 9, of which 5 were waited for; matrix products, arithmetic and copies ran while one was open for 0% of the time, Pallas kernels for 2%

profile of v4, /device:TPU:1, one launch (start us, length us, event | category | flops | bytes accessed | tf_op | source)
XLA Modules:
  0.0 115.4 jit_solution(18356068244164972791)
XLA Ops:
  0.0 1.2 %copy-done = f32[1,1,512,512]{3,2,1,0:T(8,128)S(1)} copy-done((f32[1,1,512,512]{3,2,1,0:T(8,128)S(1)}, f32[1,1,512,512]{3,2,1,0:T(8,128)}, u32[]{:S(2)}) %copy-start) | copy-done | bytes 1048600
  1.2 0.7 pack_statistic.1
  2.0 24.3 %all-to-all-start = ((bf16[512,2,128]{2,1,0:T(2,128)(2,1)}), bf16[512,2,128]{2,1,0:T(2,128)(2,1)S(1)}, u32[]{:S(2)}, u32[]{:S(2)}) async-start(bf16[512,2,128]{2,1,0:T(2,128)(2,1)} %bitcast.7), calls=%async_computation | async-start | bytes 524288 | tf_op jit(solution)/shard_map/all_to_all | solution.py:254
  26.4 0.6 part_columns.1
  27.0 3.3 %collective-permute-start = (bf16[4,64,512]{2,1,0:T(8,128)(2,1)S(1)}, bf16[4,64,512]{2,1,0:T(8,128)(2,1)S(1)}, u32[]{:S(2)}, u32[]{:S(2)}) collective-permute-start(bf16[4,64,512]{2,1,0:T(8,128)(2,1)S(1)} %get-tuple-element.17), channel_id=1, source_target_pairs={{0,1},{1,2},{2,3},{3,0},{4,5},{5,6},{6,7},{7,4},{8,9},{9,10},{10,1... | collective-permute-start | bytes 786440 | tf_op jit(solution)/shard_map/ppermute | solution.py:250
  30.3 3.2 %collective-permute-start.1 = (bf16[4,64,512]{2,1,0:T(8,128)(2,1)S(1)}, bf16[4,64,512]{2,1,0:T(8,128)(2,1)S(1)}, u32[]{:S(2)}, u32[]{:S(2)}) collective-permute-start(bf16[4,64,512]{2,1,0:T(8,128)(2,1)S(1)} %get-tuple-element.18), channel_id=1, source_target_pairs={{0,3},{1,0},{2,1},{3,2},{4,7},{5,4},{6,5},{7,6},{8,11},{9,8},{10,9... | collective-permute-start | bytes 786440 | tf_op jit(solution)/shard_map/ppermute | solution.py:250
  33.8 2.5 %collective-permute-done = bf16[4,64,512]{2,1,0:T(8,128)(2,1)S(1)} collective-permute-done((bf16[4,64,512]{2,1,0:T(8,128)(2,1)S(1)}, bf16[4,64,512]{2,1,0:T(8,128)(2,1)S(1)}, u32[]{:S(2)}, u32[]{:S(2)}) %collective-permute-start) | collective-permute-done | bytes 262176 | tf_op jit(solution)/shard_map/ppermute | solution.py:250
  36.3 2.2 %collective-permute-done.1 = bf16[4,64,512]{2,1,0:T(8,128)(2,1)S(1)} collective-permute-done((bf16[4,64,512]{2,1,0:T(8,128)(2,1)S(1)}, bf16[4,64,512]{2,1,0:T(8,128)(2,1)S(1)}, u32[]{:S(2)}, u32[]{:S(2)}) %collective-permute-start.1) | collective-permute-done | bytes 262176 | tf_op jit(solution)/shard_map/ppermute | solution.py:250
  38.6 12.4 %all-to-all-done.table_ref = bf16[512,2,128]{2,1,0:T(2,128)(2,1)S(1)} async-done(((bf16[512,2,128]{2,1,0:T(2,128)(2,1)}), bf16[512,2,128]{2,1,0:T(2,128)(2,1)S(1)}, u32[]{:S(2)}, u32[]{:S(2)}) %all-to-all-start) | async-done | bytes 262176 | tf_op jit(solution)/shard_map/all_to_all | solution.py:254
  51.0 1.6 %select_rows.1 = bf16[576,2,128]{2,1,0:T(2,128)(2,1)} custom-call(s32[512]{0:T(512)S(1)} %fusion.1.source_ref, bf16[512,2,128]{2,1,0:T(2,128)(2,1)S(1)} %all-to-all-done.table_ref, f32[1,256]{1,0:T(1,128)S(1)} %get-tuple-element.20.diagonal_ref), custom_call_target="tpu_custom_call" | custom-call | tf_op jit(solution)/shard_map/select_rows/pallas_call | solution.py:98
  52.5 5.6 %all-to-all-start.1 = ((bf16[576,2,128]{2,1,0:T(2,128)(2,1)}), bf16[576,2,128]{2,1,0:T(2,128)(2,1)S(1)}, u32[]{:S(2)}, u32[]{:S(2)}) async-start(bf16[576,2,128]{2,1,0:T(2,128)(2,1)} %select_rows.1), calls=%async_computation.1 | async-start | bytes 589824 | tf_op jit(solution)/shard_map/all_to_all | solution.py:260
  58.1 4.3 %collective-permute-start.2 = (bf16[4,64,512]{2,1,0:T(8,128)(2,1)S(1)}, bf16[4,64,512]{2,1,0:T(8,128)(2,1)S(1)}, u32[]{:S(2)}, u32[]{:S(2)}) collective-permute-start(bf16[4,64,512]{2,1,0:T(8,128)(2,1)S(1)} %get-tuple-element.23), channel_id=1, source_target_pairs={{0,2},{1,3},{2,0},{3,1},{4,6},{5,7},{6,4},{7,5},{8,10},{9,11},{10,... | collective-permute-start | bytes 786440 | tf_op jit(solution)/shard_map/ppermute | solution.py:250
  62.5 5.2 %collective-permute-done.2 = bf16[4,64,512]{2,1,0:T(8,128)(2,1)S(1)} collective-permute-done((bf16[4,64,512]{2,1,0:T(8,128)(2,1)S(1)}, bf16[4,64,512]{2,1,0:T(8,128)(2,1)S(1)}, u32[]{:S(2)}, u32[]{:S(2)}) %collective-permute-start.2) | collective-permute-done | bytes 262176 | tf_op jit(solution)/shard_map/ppermute | solution.py:250
  67.8 2.6 %collective-permute-start.3 = (bf16[64,512]{1,0:T(8,128)(2,1)S(1)}, bf16[64,512]{1,0:T(8,128)(2,1)S(1)}, u32[]{:S(2)}, u32[]{:S(2)}) collective-permute-start(bf16[64,512]{1,0:T(8,128)(2,1)S(1)} %get-tuple-element.30), channel_id=1, source_target_pairs={{0,8},{8,16},{16,24},{24,0},{1,9},{9,17},{17,25},{25,1},{2,10},{10... | collective-permute-start | bytes 196616 | tf_op jit(solution)/shard_map/ppermute | solution.py:266
  70.5 4.0 %collective-permute-start.4 = (bf16[64,512]{1,0:T(8,128)(2,1)S(1)}, bf16[64,512]{1,0:T(8,128)(2,1)S(1)}, u32[]{:S(2)}, u32[]{:S(2)}) collective-permute-start(bf16[64,512]{1,0:T(8,128)(2,1)S(1)} %get-tuple-element.29), channel_id=1, source_target_pairs={{0,16},{8,24},{16,0},{24,8},{1,17},{9,25},{17,1},{25,9},{2,18},{10... | collective-permute-start | bytes 196616 | tf_op jit(solution)/shard_map/ppermute | solution.py:266
  74.5 3.1 %collective-permute-start.5 = (bf16[64,512]{1,0:T(8,128)(2,1)S(1)}, bf16[64,512]{1,0:T(8,128)(2,1)S(1)}, u32[]{:S(2)}, u32[]{:S(2)}) collective-permute-start(bf16[64,512]{1,0:T(8,128)(2,1)S(1)} %get-tuple-element.28), channel_id=1, source_target_pairs={{0,24},{8,0},{16,8},{24,16},{1,25},{9,1},{17,9},{25,17},{2,26},{10... | collective-permute-start | bytes 196616 | tf_op jit(solution)/shard_map/ppermute | solution.py:266
  77.6 0.1 all-to-all-done.1.table_ref
  77.7 1.6 %regroup.1 = bf16[4,144,2,128]{3,2,1,0:T(2,128)(2,1)} custom-call(s32[4]{0:T(128)S(1)} %pad_add_fusion.place_ref, s32[512]{0:T(512)S(1)} %add.47.source_ref, bf16[576,2,128]{2,1,0:T(2,128)(2,1)S(1)} %all-to-all-done.1.table_ref), custom_call_target="tpu_custom_call" | custom-call | tf_op jit(solution)/shard_map/regroup/pallas_call | solution.py:136
  79.3 3.8 %all-to-all-start.2 = ((bf16[4,144,2,128]{3,2,1,0:T(2,128)(2,1)}), bf16[4,144,2,128]{3,2,1,0:T(2,128)(2,1)S(1)}, u32[]{:S(2)}, u32[]{:S(2)}) async-start(bf16[4,144,2,128]{3,2,1,0:T(2,128)(2,1)} %regroup.1), calls=%async_computation.2 | async-start | bytes 589824 | tf_op jit(solution)/shard_map/all_to_all | solution.py:272
  83.2 5.9 %all-gather = bf16[8,64,512]{2,1,0:T(8,128)(2,1)S(1)} all-gather(bf16[4,64,512]{2,1,0:T(8,128)(2,1)S(1)} %pad_maximum_fusion), channel_id=2, replica_groups=mesh['y'=4,'zq'=4,'zl'=4,'core'=2,'rep'=4] {'core'}, dimensions={0}, use_global_device_ids=true | all-gather | bytes 786432 | tf_op jit(solution)/shard_map/all_gather | solution.py:268
  89.1 6.8 %all_gather.9.packed_ref = bf16[2,4,72,512]{3,2,1,0:T(8,128)(2,1)S(1)} all-gather(bf16[1,4,72,512]{3,2,1,0:T(8,128)(2,1)S(1)} %bitcast.32), channel_id=1, replica_groups=mesh['y'=4,'zq'=4,'zl'=4,'core'=2,'rep'=4] {'core'}, dimensions={0}, use_global_device_ids=true | all-gather | bytes 884736 | tf_op jit(solution)/shard_map/all_gather | solution.py:275
  96.0 6.1 %precondition.1 = bf16[4,64,512]{2,1,0:T(8,128)(2,1)S(1)} custom-call(s32[4]{0:T(128)S(1)} %pad_add_fusion.place_ref, bf16[2,4,72,512]{3,2,1,0:T(8,128)(2,1)S(1)} %all_gather.9.packed_ref, bf16[2,4,64,512]{3,2,1,0:T(8,128)(2,1)S(1)} %bitcast.29), custom_call_target="tpu_custom_call" | custom-call | tf_op jit(solution)/shard_map/precondition/pallas_call | solution.py:220
  102.0 12.7 %all_to_all.20 = bf16[16,16,512]{2,1,0:T(8,128)(2,1)S(1)} all-to-all(bf16[16,16,512]{2,1,0:T(8,128)(2,1)S(1)} %bitcast.30), channel_id=1, replica_groups=mesh['y'=4,'zq'=4,'zl'=4,'core'=2,'rep'=4] {'zl','rep'}, dimensions={0} | all-to-all | bytes 524288 | tf_op jit(solution)/shard_map/all_to_all | solution.py:279
  114.7 0.7 copy.13
  (18 shorter events, 0.6 us)
Async XLA Ops:
  0.0 1.2 %copy-start = (f32[1,1,512,512]{3,2,1,0:T(8,128)S(1)}, f32[1,1,512,512]{3,2,1,0:T(8,128)}, u32[]{:S(2)}) copy-start(f32[1,1,512,512]{3,2,1,0:T(8,128)} %param.4) | copy-start | bytes 3145732
  1.2 25.2 %copy-start.1 = (bf16[1,64,8192]{2,1,0:T(8,128)(2,1)S(1)}, bf16[1,64,8192]{2,1,0:T(8,128)(2,1)}, u32[]{:S(2)}) copy-start(bf16[1,64,8192]{2,1,0:T(8,128)(2,1)} %partial_ref.1) | copy-start | bytes 3145732
  2.0 49.0 %all-to-all-start = ((bf16[512,2,128]{2,1,0:T(2,128)(2,1)}), bf16[512,2,128]{2,1,0:T(2,128)(2,1)S(1)}, u32[]{:S(2)}, u32[]{:S(2)}) async-start(bf16[512,2,128]{2,1,0:T(2,128)(2,1)} %bitcast.7), calls=%async_computation | async-start | bytes 524288 | tf_op jit(solution)/shard_map/all_to_all | solution.py:254
  27.0 6.5 %copy-start.2 = (s32[256]{0:T(256)S(1)}, s32[256]{0:T(256)}, u32[]{:S(2)}) copy-start(s32[256]{0:T(256)} %param.5) | copy-start | bytes 3076
  27.0 9.3 %collective-permute-start = (bf16[4,64,512]{2,1,0:T(8,128)(2,1)S(1)}, bf16[4,64,512]{2,1,0:T(8,128)(2,1)S(1)}, u32[]{:S(2)}, u32[]{:S(2)}) collective-permute-start(bf16[4,64,512]{2,1,0:T(8,128)(2,1)S(1)} %get-tuple-element.17), channel_id=1, source_target_pairs={{0,1},{1,2},{2,3},{3,0},{4,5},{5,6},{6,7},{7,4},{8,9},{9,10},{10,1... | collective-permute-start | bytes 786440 | tf_op jit(solution)/shard_map/ppermute | solution.py:250
  30.3 8.2 %collective-permute-start.1 = (bf16[4,64,512]{2,1,0:T(8,128)(2,1)S(1)}, bf16[4,64,512]{2,1,0:T(8,128)(2,1)S(1)}, u32[]{:S(2)}, u32[]{:S(2)}) collective-permute-start(bf16[4,64,512]{2,1,0:T(8,128)(2,1)S(1)} %get-tuple-element.18), channel_id=1, source_target_pairs={{0,3},{1,0},{2,1},{3,2},{4,7},{5,4},{6,5},{7,6},{8,11},{9,8},{10,9... | collective-permute-start | bytes 786440 | tf_op jit(solution)/shard_map/ppermute | solution.py:250
  52.5 25.2 %all-to-all-start.1 = ((bf16[576,2,128]{2,1,0:T(2,128)(2,1)}), bf16[576,2,128]{2,1,0:T(2,128)(2,1)S(1)}, u32[]{:S(2)}, u32[]{:S(2)}) async-start(bf16[576,2,128]{2,1,0:T(2,128)(2,1)} %select_rows.1), calls=%async_computation.1 | async-start | bytes 589824 | tf_op jit(solution)/shard_map/all_to_all | solution.py:260
  58.1 9.6 %collective-permute-start.2 = (bf16[4,64,512]{2,1,0:T(8,128)(2,1)S(1)}, bf16[4,64,512]{2,1,0:T(8,128)(2,1)S(1)}, u32[]{:S(2)}, u32[]{:S(2)}) collective-permute-start(bf16[4,64,512]{2,1,0:T(8,128)(2,1)S(1)} %get-tuple-element.23), channel_id=1, source_target_pairs={{0,2},{1,3},{2,0},{3,1},{4,6},{5,7},{6,4},{7,5},{8,10},{9,11},{10,... | collective-permute-start | bytes 786440 | tf_op jit(solution)/shard_map/ppermute | solution.py:250
  67.8 9.7 %collective-permute-start.3 = (bf16[64,512]{1,0:T(8,128)(2,1)S(1)}, bf16[64,512]{1,0:T(8,128)(2,1)S(1)}, u32[]{:S(2)}, u32[]{:S(2)}) collective-permute-start(bf16[64,512]{1,0:T(8,128)(2,1)S(1)} %get-tuple-element.30), channel_id=1, source_target_pairs={{0,8},{8,16},{16,24},{24,0},{1,9},{9,17},{17,25},{25,1},{2,10},{10... | collective-permute-start | bytes 196616 | tf_op jit(solution)/shard_map/ppermute | solution.py:266
  70.5 12.6 %collective-permute-start.4 = (bf16[64,512]{1,0:T(8,128)(2,1)S(1)}, bf16[64,512]{1,0:T(8,128)(2,1)S(1)}, u32[]{:S(2)}, u32[]{:S(2)}) collective-permute-start(bf16[64,512]{1,0:T(8,128)(2,1)S(1)} %get-tuple-element.29), channel_id=1, source_target_pairs={{0,16},{8,24},{16,0},{24,8},{1,17},{9,25},{17,1},{25,9},{2,18},{10... | collective-permute-start | bytes 196616 | tf_op jit(solution)/shard_map/ppermute | solution.py:266
  74.5 8.7 %collective-permute-start.5 = (bf16[64,512]{1,0:T(8,128)(2,1)S(1)}, bf16[64,512]{1,0:T(8,128)(2,1)S(1)}, u32[]{:S(2)}, u32[]{:S(2)}) collective-permute-start(bf16[64,512]{1,0:T(8,128)(2,1)S(1)} %get-tuple-element.28), channel_id=1, source_target_pairs={{0,24},{8,0},{16,8},{24,16},{1,25},{9,1},{17,9},{25,17},{2,26},{10... | collective-permute-start | bytes 196616 | tf_op jit(solution)/shard_map/ppermute | solution.py:266
  79.3 9.8 %all-to-all-start.2 = ((bf16[4,144,2,128]{3,2,1,0:T(2,128)(2,1)}), bf16[4,144,2,128]{3,2,1,0:T(2,128)(2,1)S(1)}, u32[]{:S(2)}, u32[]{:S(2)}) async-start(bf16[4,144,2,128]{3,2,1,0:T(2,128)(2,1)} %regroup.1), calls=%async_computation.2 | async-start | bytes 589824 | tf_op jit(solution)/shard_map/all_to_all | solution.py:272

commit v5 on v4

--- a/solution.py
+++ b/solution.py
@@ -118,7 +118,7 @@
                 out_ref[rep, side * rows + index] = piece
         return carry
 
-    lax.fori_loop(0, rows, body, 0, unroll=4)
+    lax.fori_loop(0, rows, body, 0, unroll=64)
     nothing = jnp.zeros((lines, lanes), F32)
     for rep in range(reps):
         for side in range(2):

time: 116 us -> 116 us (level)
  no operation moved by 1% of the time
where the time goes in v5:
time: 116 us; the launch traced here: 115 us
  starting transfers between devices  54.2 us (47%)
  blocking collectives  25.4 us (22%)
  waiting for transfers between devices  22.5 us (19%)
  Pallas kernels  10.5 us (9%)
  local copies, waits for them, and re-layouts  2.2 us (2%)
    all_to_all x1, starting transfers between devices, on_device(): lax.all_to_all(tiles.reshape(everyone, 2, 128), ACROSS, split_axis=0, con...  24.3 us
    all_to_all x1, blocking collectives, on_device(): lax.all_to_all(update, ('zl', 'rep'), split_axis=0, concat_axis=0, tiled=...  12.6 us
    all_to_all x1, waiting for transfers between devices, on_device(): lax.all_to_all(tiles.reshape(everyone, 2, 128), ACROSS, split_axis=0, con...  12.4 us
    ppermute x3, starting transfers between devices, on_device(): parts[step] = lax.ppermute(parts[step], 'rep', route)  10.8 us
    ppermute x3, waiting for transfers between devices, on_device(): parts[step] = lax.ppermute(parts[step], 'rep', route)  9.93 us
    ppermute x3, starting transfers between devices, on_device(): pieces.append(lax.ppermute(summed[step], 'zl', route))  9.72 us
    all_gather x1, blocking collectives, on_device(): delivered = lax.all_gather(delivered, 'core')  6.83 us
    pallas_call x1, Pallas kernels, precondition(): pl.pallas_call(main_kernel, out_shape=jax.ShapeDtypeStruct(pieces.shape[1...  6.06 us
  transfers between devices with their start and end apart: 9, of which 5 were waited for; matrix products, arithmetic and copies ran while one was open for 0% of the time, Pallas kernels for 2%

profile of v5, /device:TPU:1, one launch (start us, length us, event | category | flops | bytes accessed | tf_op | source)
XLA Modules:
  0.0 115.3 jit_solution(5468554494669026436)
XLA Ops:
  0.0 1.2 %copy-done = f32[1,1,512,512]{3,2,1,0:T(8,128)S(1)} copy-done((f32[1,1,512,512]{3,2,1,0:T(8,128)S(1)}, f32[1,1,512,512]{3,2,1,0:T(8,128)}, u32[]{:S(2)}) %copy-start) | copy-done | bytes 1048600
  1.2 0.7 pack_statistic.1
  2.0 24.3 %all-to-all-start = ((bf16[512,2,128]{2,1,0:T(2,128)(2,1)}), bf16[512,2,128]{2,1,0:T(2,128)(2,1)S(1)}, u32[]{:S(2)}, u32[]{:S(2)}) async-start(bf16[512,2,128]{2,1,0:T(2,128)(2,1)} %bitcast.7), calls=%async_computation | async-start | bytes 524288 | tf_op jit(solution)/shard_map/all_to_all | solution.py:254
  26.4 0.6 part_columns.1
  27.0 3.3 %collective-permute-start = (bf16[4,64,512]{2,1,0:T(8,128)(2,1)S(1)}, bf16[4,64,512]{2,1,0:T(8,128)(2,1)S(1)}, u32[]{:S(2)}, u32[]{:S(2)}) collective-permute-start(bf16[4,64,512]{2,1,0:T(8,128)(2,1)S(1)} %get-tuple-element.17), channel_id=1, source_target_pairs={{0,1},{1,2},{2,3},{3,0},{4,5},{5,6},{6,7},{7,4},{8,9},{9,10},{10,1... | collective-permute-start | bytes 786440 | tf_op jit(solution)/shard_map/ppermute | solution.py:250
  30.3 3.2 %collective-permute-start.1 = (bf16[4,64,512]{2,1,0:T(8,128)(2,1)S(1)}, bf16[4,64,512]{2,1,0:T(8,128)(2,1)S(1)}, u32[]{:S(2)}, u32[]{:S(2)}) collective-permute-start(bf16[4,64,512]{2,1,0:T(8,128)(2,1)S(1)} %get-tuple-element.18), channel_id=1, source_target_pairs={{0,3},{1,0},{2,1},{3,2},{4,7},{5,4},{6,5},{7,6},{8,11},{9,8},{10,9... | collective-permute-start | bytes 786440 | tf_op jit(solution)/shard_map/ppermute | solution.py:250
  33.8 2.5 %collective-permute-done = bf16[4,64,512]{2,1,0:T(8,128)(2,1)S(1)} collective-permute-done((bf16[4,64,512]{2,1,0:T(8,128)(2,1)S(1)}, bf16[4,64,512]{2,1,0:T(8,128)(2,1)S(1)}, u32[]{:S(2)}, u32[]{:S(2)}) %collective-permute-start) | collective-permute-done | bytes 262176 | tf_op jit(solution)/shard_map/ppermute | solution.py:250
  36.3 2.2 %collective-permute-done.1 = bf16[4,64,512]{2,1,0:T(8,128)(2,1)S(1)} collective-permute-done((bf16[4,64,512]{2,1,0:T(8,128)(2,1)S(1)}, bf16[4,64,512]{2,1,0:T(8,128)(2,1)S(1)}, u32[]{:S(2)}, u32[]{:S(2)}) %collective-permute-start.1) | collective-permute-done | bytes 262176 | tf_op jit(solution)/shard_map/ppermute | solution.py:250
  38.6 12.4 %all-to-all-done.table_ref = bf16[512,2,128]{2,1,0:T(2,128)(2,1)S(1)} async-done(((bf16[512,2,128]{2,1,0:T(2,128)(2,1)}), bf16[512,2,128]{2,1,0:T(2,128)(2,1)S(1)}, u32[]{:S(2)}, u32[]{:S(2)}) %all-to-all-start) | async-done | bytes 262176 | tf_op jit(solution)/shard_map/all_to_all | solution.py:254
  51.0 1.6 %select_rows.1 = bf16[576,2,128]{2,1,0:T(2,128)(2,1)} custom-call(s32[512]{0:T(512)S(1)} %fusion.1.source_ref, bf16[512,2,128]{2,1,0:T(2,128)(2,1)S(1)} %all-to-all-done.table_ref, f32[1,256]{1,0:T(1,128)S(1)} %get-tuple-element.20.diagonal_ref), custom_call_target="tpu_custom_call" | custom-call | tf_op jit(solution)/shard_map/select_rows/pallas_call | solution.py:98
  52.5 5.6 %all-to-all-start.1 = ((bf16[576,2,128]{2,1,0:T(2,128)(2,1)}), bf16[576,2,128]{2,1,0:T(2,128)(2,1)S(1)}, u32[]{:S(2)}, u32[]{:S(2)}) async-start(bf16[576,2,128]{2,1,0:T(2,128)(2,1)} %select_rows.1), calls=%async_computation.1 | async-start | bytes 589824 | tf_op jit(solution)/shard_map/all_to_all | solution.py:260
  58.1 4.3 %collective-permute-start.2 = (bf16[4,64,512]{2,1,0:T(8,128)(2,1)S(1)}, bf16[4,64,512]{2,1,0:T(8,128)(2,1)S(1)}, u32[]{:S(2)}, u32[]{:S(2)}) collective-permute-start(bf16[4,64,512]{2,1,0:T(8,128)(2,1)S(1)} %get-tuple-element.23), channel_id=1, source_target_pairs={{0,2},{1,3},{2,0},{3,1},{4,6},{5,7},{6,4},{7,5},{8,10},{9,11},{10,... | collective-permute-start | bytes 786440 | tf_op jit(solution)/shard_map/ppermute | solution.py:250
  62.5 5.2 %collective-permute-done.2 = bf16[4,64,512]{2,1,0:T(8,128)(2,1)S(1)} collective-permute-done((bf16[4,64,512]{2,1,0:T(8,128)(2,1)S(1)}, bf16[4,64,512]{2,1,0:T(8,128)(2,1)S(1)}, u32[]{:S(2)}, u32[]{:S(2)}) %collective-permute-start.2) | collective-permute-done | bytes 262176 | tf_op jit(solution)/shard_map/ppermute | solution.py:250
  67.8 2.6 %collective-permute-start.3 = (bf16[64,512]{1,0:T(8,128)(2,1)S(1)}, bf16[64,512]{1,0:T(8,128)(2,1)S(1)}, u32[]{:S(2)}, u32[]{:S(2)}) collective-permute-start(bf16[64,512]{1,0:T(8,128)(2,1)S(1)} %get-tuple-element.30), channel_id=1, source_target_pairs={{0,8},{8,16},{16,24},{24,0},{1,9},{9,17},{17,25},{25,1},{2,10},{10... | collective-permute-start | bytes 196616 | tf_op jit(solution)/shard_map/ppermute | solution.py:266
  70.5 4.0 %collective-permute-start.4 = (bf16[64,512]{1,0:T(8,128)(2,1)S(1)}, bf16[64,512]{1,0:T(8,128)(2,1)S(1)}, u32[]{:S(2)}, u32[]{:S(2)}) collective-permute-start(bf16[64,512]{1,0:T(8,128)(2,1)S(1)} %get-tuple-element.29), channel_id=1, source_target_pairs={{0,16},{8,24},{16,0},{24,8},{1,17},{9,25},{17,1},{25,9},{2,18},{10... | collective-permute-start | bytes 196616 | tf_op jit(solution)/shard_map/ppermute | solution.py:266
  74.5 3.1 %collective-permute-start.5 = (bf16[64,512]{1,0:T(8,128)(2,1)S(1)}, bf16[64,512]{1,0:T(8,128)(2,1)S(1)}, u32[]{:S(2)}, u32[]{:S(2)}) collective-permute-start(bf16[64,512]{1,0:T(8,128)(2,1)S(1)} %get-tuple-element.28), channel_id=1, source_target_pairs={{0,24},{8,0},{16,8},{24,16},{1,25},{9,1},{17,9},{25,17},{2,26},{10... | collective-permute-start | bytes 196616 | tf_op jit(solution)/shard_map/ppermute | solution.py:266
  77.6 0.1 all-to-all-done.1.table_ref
  77.7 1.5 %regroup.1 = bf16[4,144,2,128]{3,2,1,0:T(2,128)(2,1)} custom-call(s32[4]{0:T(128)S(1)} %pad_add_fusion.place_ref, s32[512]{0:T(512)S(1)} %add.47.source_ref, bf16[576,2,128]{2,1,0:T(2,128)(2,1)S(1)} %all-to-all-done.1.table_ref), custom_call_target="tpu_custom_call" | custom-call | tf_op jit(solution)/shard_map/regroup/pallas_call | solution.py:136
  79.2 3.8 %all-to-all-start.2 = ((bf16[4,144,2,128]{3,2,1,0:T(2,128)(2,1)}), bf16[4,144,2,128]{3,2,1,0:T(2,128)(2,1)S(1)}, u32[]{:S(2)}, u32[]{:S(2)}) async-start(bf16[4,144,2,128]{3,2,1,0:T(2,128)(2,1)} %regroup.1), calls=%async_computation.2 | async-start | bytes 589824 | tf_op jit(solution)/shard_map/all_to_all | solution.py:272
  83.1 5.9 %all-gather = bf16[8,64,512]{2,1,0:T(8,128)(2,1)S(1)} all-gather(bf16[4,64,512]{2,1,0:T(8,128)(2,1)S(1)} %pad_maximum_fusion), channel_id=2, replica_groups=mesh['y'=4,'zq'=4,'zl'=4,'core'=2,'rep'=4] {'core'}, dimensions={0}, use_global_device_ids=true | all-gather | bytes 786432 | tf_op jit(solution)/shard_map/all_gather | solution.py:268
  89.1 6.8 %all_gather.9.packed_ref = bf16[2,4,72,512]{3,2,1,0:T(8,128)(2,1)S(1)} all-gather(bf16[1,4,72,512]{3,2,1,0:T(8,128)(2,1)S(1)} %bitcast.32), channel_id=1, replica_groups=mesh['y'=4,'zq'=4,'zl'=4,'core'=2,'rep'=4] {'core'}, dimensions={0}, use_global_device_ids=true | all-gather | bytes 884736 | tf_op jit(solution)/shard_map/all_gather | solution.py:275
  95.9 6.1 %precondition.1 = bf16[4,64,512]{2,1,0:T(8,128)(2,1)S(1)} custom-call(s32[4]{0:T(128)S(1)} %pad_add_fusion.place_ref, bf16[2,4,72,512]{3,2,1,0:T(8,128)(2,1)S(1)} %all_gather.9.packed_ref, bf16[2,4,64,512]{3,2,1,0:T(8,128)(2,1)S(1)} %bitcast.29), custom_call_target="tpu_custom_call" | custom-call | tf_op jit(solution)/shard_map/precondition/pallas_call | solution.py:220
  102.0 12.6 %all_to_all.20 = bf16[16,16,512]{2,1,0:T(8,128)(2,1)S(1)} all-to-all(bf16[16,16,512]{2,1,0:T(8,128)(2,1)S(1)} %bitcast.30), channel_id=1, replica_groups=mesh['y'=4,'zq'=4,'zl'=4,'core'=2,'rep'=4] {'zl','rep'}, dimensions={0} | all-to-all | bytes 524288 | tf_op jit(solution)/shard_map/all_to_all | solution.py:279
  114.6 0.7 copy.13
  (18 shorter events, 0.6 us)
Async XLA Ops:
  0.0 1.2 %copy-start = (f32[1,1,512,512]{3,2,1,0:T(8,128)S(1)}, f32[1,1,512,512]{3,2,1,0:T(8,128)}, u32[]{:S(2)}) copy-start(f32[1,1,512,512]{3,2,1,0:T(8,128)} %param.4) | copy-start | bytes 3145732
  1.2 25.2 %copy-start.1 = (bf16[1,64,8192]{2,1,0:T(8,128)(2,1)S(1)}, bf16[1,64,8192]{2,1,0:T(8,128)(2,1)}, u32[]{:S(2)}) copy-start(bf16[1,64,8192]{2,1,0:T(8,128)(2,1)} %partial_ref.1) | copy-start | bytes 3145732
  2.0 49.0 %all-to-all-start = ((bf16[512,2,128]{2,1,0:T(2,128)(2,1)}), bf16[512,2,128]{2,1,0:T(2,128)(2,1)S(1)}, u32[]{:S(2)}, u32[]{:S(2)}) async-start(bf16[512,2,128]{2,1,0:T(2,128)(2,1)} %bitcast.7), calls=%async_computation | async-start | bytes 524288 | tf_op jit(solution)/shard_map/all_to_all | solution.py:254
  27.0 6.5 %copy-start.2 = (s32[256]{0:T(256)S(1)}, s32[256]{0:T(256)}, u32[]{:S(2)}) copy-start(s32[256]{0:T(256)} %param.5) | copy-start | bytes 3076
  27.0 9.3 %collective-permute-start = (bf16[4,64,512]{2,1,0:T(8,128)(2,1)S(1)}, bf16[4,64,512]{2,1,0:T(8,128)(2,1)S(1)}, u32[]{:S(2)}, u32[]{:S(2)}) collective-permute-start(bf16[4,64,512]{2,1,0:T(8,128)(2,1)S(1)} %get-tuple-element.17), channel_id=1, source_target_pairs={{0,1},{1,2},{2,3},{3,0},{4,5},{5,6},{6,7},{7,4},{8,9},{9,10},{10,1... | collective-permute-start | bytes 786440 | tf_op jit(solution)/shard_map/ppermute | solution.py:250
  30.3 8.2 %collective-permute-start.1 = (bf16[4,64,512]{2,1,0:T(8,128)(2,1)S(1)}, bf16[4,64,512]{2,1,0:T(8,128)(2,1)S(1)}, u32[]{:S(2)}, u32[]{:S(2)}) collective-permute-start(bf16[4,64,512]{2,1,0:T(8,128)(2,1)S(1)} %get-tuple-element.18), channel_id=1, source_target_pairs={{0,3},{1,0},{2,1},{3,2},{4,7},{5,4},{6,5},{7,6},{8,11},{9,8},{10,9... | collective-permute-start | bytes 786440 | tf_op jit(solution)/shard_map/ppermute | solution.py:250
  52.5 25.2 %all-to-all-start.1 = ((bf16[576,2,128]{2,1,0:T(2,128)(2,1)}), bf16[576,2,128]{2,1,0:T(2,128)(2,1)S(1)}, u32[]{:S(2)}, u32[]{:S(2)}) async-start(bf16[576,2,128]{2,1,0:T(2,128)(2,1)} %select_rows.1), calls=%async_computation.1 | async-start | bytes 589824 | tf_op jit(solution)/shard_map/all_to_all | solution.py:260
  58.1 9.6 %collective-permute-start.2 = (bf16[4,64,512]{2,1,0:T(8,128)(2,1)S(1)}, bf16[4,64,512]{2,1,0:T(8,128)(2,1)S(1)}, u32[]{:S(2)}, u32[]{:S(2)}) collective-permute-start(bf16[4,64,512]{2,1,0:T(8,128)(2,1)S(1)} %get-tuple-element.23), channel_id=1, source_target_pairs={{0,2},{1,3},{2,0},{3,1},{4,6},{5,7},{6,4},{7,5},{8,10},{9,11},{10,... | collective-permute-start | bytes 786440 | tf_op jit(solution)/shard_map/ppermute | solution.py:250
  67.8 9.7 %collective-permute-start.3 = (bf16[64,512]{1,0:T(8,128)(2,1)S(1)}, bf16[64,512]{1,0:T(8,128)(2,1)S(1)}, u32[]{:S(2)}, u32[]{:S(2)}) collective-permute-start(bf16[64,512]{1,0:T(8,128)(2,1)S(1)} %get-tuple-element.30), channel_id=1, source_target_pairs={{0,8},{8,16},{16,24},{24,0},{1,9},{9,17},{17,25},{25,1},{2,10},{10... | collective-permute-start | bytes 196616 | tf_op jit(solution)/shard_map/ppermute | solution.py:266
  70.5 12.6 %collective-permute-start.4 = (bf16[64,512]{1,0:T(8,128)(2,1)S(1)}, bf16[64,512]{1,0:T(8,128)(2,1)S(1)}, u32[]{:S(2)}, u32[]{:S(2)}) collective-permute-start(bf16[64,512]{1,0:T(8,128)(2,1)S(1)} %get-tuple-element.29), channel_id=1, source_target_pairs={{0,16},{8,24},{16,0},{24,8},{1,17},{9,25},{17,1},{25,9},{2,18},{10... | collective-permute-start | bytes 196616 | tf_op jit(solution)/shard_map/ppermute | solution.py:266
  74.5 8.6 %collective-permute-start.5 = (bf16[64,512]{1,0:T(8,128)(2,1)S(1)}, bf16[64,512]{1,0:T(8,128)(2,1)S(1)}, u32[]{:S(2)}, u32[]{:S(2)}) collective-permute-start(bf16[64,512]{1,0:T(8,128)(2,1)S(1)} %get-tuple-element.28), channel_id=1, source_target_pairs={{0,24},{8,0},{16,8},{24,16},{1,25},{9,1},{17,9},{25,17},{2,26},{10... | collective-permute-start | bytes 196616 | tf_op jit(solution)/shard_map/ppermute | solution.py:266
  79.2 9.8 %all-to-all-start.2 = ((bf16[4,144,2,128]{3,2,1,0:T(2,128)(2,1)}), bf16[4,144,2,128]{3,2,1,0:T(2,128)(2,1)S(1)}, u32[]{:S(2)}, u32[]{:S(2)}) async-start(bf16[4,144,2,128]{3,2,1,0:T(2,128)(2,1)} %regroup.1), calls=%async_computation.2 | async-start | bytes 589824 | tf_op jit(solution)/shard_map/all_to_all | solution.py:272
